TPU v7x, 32 devices: a whole 2x2x4 slice. The times are simulated.
32 devices in a mesh: dp: 8 (over z, y), mp: 4 (over x, core).
Axes of the slice: x: 2, y: 2, z: 4, core: 2. Of those that a mesh axis runs over, the one named last changes fastest.
Arguments:
- latents: bfloat16 [5120, 1280], P('dp', 'mp'), may hold values from -8 to 8
- time_embed: bfloat16 [20, 1280], replicated, may hold values from -6 to 6
- text_states: bfloat16 [8, 77, 2048], replicated, may hold values from -6 to 6
- item_prompt: int32 [20], replicated, may hold values from 0 to 7
- prompt_length: int32 [8], replicated, may hold values from 1 to 77
- out_grad: bfloat16 [5120, 1280], P('dp', 'mp'), may hold values from -6 to 6
- resnorm_gain_a: float32 [1280], P('mp'), may hold values from 0.5 to 1.5
- resnorm_bias_a: float32 [1280], P('mp'), may hold values from -1.8 to 1.8
- conv_weight_a: bfloat16 [9, 1280, 1280], P(None, 'dp', 'mp'), may hold values from -0.0546875 to 0.0546875
- conv_bias_a: float32 [1280], P('mp'), may hold values from -1.8 to 1.8
- time_weight: bfloat16 [1280, 1280], P('dp', 'mp'), may hold values from -0.15625 to 0.15625
- time_bias: float32 [1280], P('mp'), may hold values from -1.8 to 1.8
- resnorm_gain_b: float32 [1280], P('mp'), may hold values from 0.5 to 1.5
- resnorm_bias_b: float32 [1280], P('mp'), may hold values from -1.8 to 1.8
- conv_weight_b: bfloat16 [9, 1280, 1280], P(None, 'dp', 'mp'), may hold values from -0.078125 to 0.078125
- conv_bias_b: float32 [1280], P('mp'), may hold values from -1.8 to 1.8
- attn_norm_gain: float32 [1280], P('mp'), may hold values from 0.5 to 1.5
- attn_norm_bias: float32 [1280], P('mp'), may hold values from -1.8 to 1.8
- qkv_weight: bfloat16 [3, 1280, 1280], P(None, 'dp', 'mp'), may hold values from -0.15625 to 0.15625
- attn_out_weight: bfloat16 [1280, 1280], P('mp', 'dp'), may hold values from -0.5 to 0.5
- attn_out_bias: float32 [1280], P('mp'), may hold values from -1.8 to 1.8
- cross_norm_gain: float32 [1280], P('mp'), may hold values from 0.5 to 1.5
- cross_norm_bias: float32 [1280], P('mp'), may hold values from -1.8 to 1.8
- cross_query_weight: bfloat16 [1280, 1280], P('dp', 'mp'), may hold values from -0.15625 to 0.15625
- cross_kv_weight: bfloat16 [2, 2048, 1280], P(None, 'dp', 'mp'), may hold values from -0.125 to 0.125
- cross_out_weight: bfloat16 [1280, 1280], P('mp', 'dp'), may hold values from -0.5 to 0.5
- cross_out_bias: float32 [1280], P('mp'), may hold values from -1.8 to 1.8
- geglu_norm_gain: float32 [1280], P('mp'), may hold values from 0.5 to 1.5
- geglu_norm_bias: float32 [1280], P('mp'), may hold values from -1.8 to 1.8
- geglu_in_weight: bfloat16 [1280, 2, 5120], P('dp', None, 'mp'), may hold values from -0.15625 to 0.15625
- geglu_in_bias: float32 [2, 5120], P(None, 'mp'), may hold values from -1.8 to 1.8
- geglu_out_weight: bfloat16 [5120, 1280], P('mp', 'dp'), may hold values from -0.078125 to 0.078125
- geglu_out_bias: float32 [1280], P('mp'), may hold values from -1.8 to 1.8
Outputs:
- block_out: bfloat16 [5120, 1280], P('dp', 'mp')
- latents_grad: float32 [5120, 1280], P('dp', 'mp')
- resnorm_gain_a_grad: float32 [1280], P('mp')
- resnorm_bias_a_grad: float32 [1280], P('mp')
- conv_weight_a_grad: float32 [9, 1280, 1280], P(None, 'dp', 'mp')
- conv_bias_a_grad: float32 [1280], P('mp')
- time_weight_grad: float32 [1280, 1280], P('dp', 'mp')
- time_bias_grad: float32 [1280], P('mp')
- resnorm_gain_b_grad: float32 [1280], P('mp')
- resnorm_bias_b_grad: float32 [1280], P('mp')
- conv_weight_b_grad: float32 [9, 1280, 1280], P(None, 'dp', 'mp')
- conv_bias_b_grad: float32 [1280], P('mp')
- attn_norm_gain_grad: float32 [1280], P('mp')
- attn_norm_bias_grad: float32 [1280], P('mp')
- qkv_weight_grad: float32 [3, 1280, 1280], P(None, 'dp', 'mp')
- attn_out_weight_grad: float32 [1280, 1280], P('mp', 'dp')
- attn_out_bias_grad: float32 [1280], P('mp')
- cross_norm_gain_grad: float32 [1280], P('mp')
- cross_norm_bias_grad: float32 [1280], P('mp')
- cross_query_weight_grad: float32 [1280, 1280], P('dp', 'mp')
- cross_kv_weight_grad: float32 [2, 2048, 1280], P(None, 'dp', 'mp')
- cross_out_weight_grad: float32 [1280, 1280], P('mp', 'dp')
- cross_out_bias_grad: float32 [1280], P('mp')
- geglu_norm_gain_grad: float32 [1280], P('mp')
- geglu_norm_bias_grad: float32 [1280], P('mp')
- geglu_in_weight_grad: float32 [1280, 2, 5120], P('dp', None, 'mp')
- geglu_in_bias_grad: float32 [2, 5120], P(None, 'mp')
- geglu_out_weight_grad: float32 [5120, 1280], P('mp', 'dp')
- geglu_out_bias_grad: float32 [1280], P('mp')
All inputs are finite; a program needn't handle non-finite values.
Results may differ from a plain program's by a relative error of at most 0.03.
Values may be sent and summed in bfloat16 or wider, within the bound.
No kernel may reach another device: no remote copies, remote signals or barrier semaphores. Data moves between devices by JAX's collectives and lax.ppermute only.
A program may use at most 384 MiB of HBM per device.

v0:
```python
import math

import jax
import jax.numpy as jnp
from jax import lax
from jax.sharding import PartitionSpec as P

C = 1280
GROUPS = 32
HEAD = 64
TXT = 2048
TEMB = 1280
TXT_LEN = 77
IMG_H = 16
IMG_W = 16
PROMPTS = 8


EPS = 1e-05
HIGH = lax.Precision.HIGHEST
NEG = -1e30


def padded_2(array, sides, width):
    for axis, dim in sides:
        size, length = (lax.axis_size(axis), array.shape[dim])
        up = [(i, (i + 1) % size) for i in range(size)]
        down = [(j, i) for i, j in up]
        last = lax.slice_in_dim(array, length - width, length, axis=dim)
        first = lax.slice_in_dim(array, 0, width, axis=dim)
        before = lax.ppermute(last, axis, up)
        after = lax.ppermute(first, axis, down)
        array = jnp.concatenate([before, array, after], axis=dim)
    return array


def narrow(array_in):
    return array_in.astype(jnp.bfloat16)


def product(operand_a, operand_b):
    return jnp.dot(operand_a, operand_b, preferred_element_type=jnp.float32)


def inner_rows(operand_a, operand_b):
    return lax.dot_general(
        operand_a, operand_b, (((0,), (0,)), ((), ())), preferred_element_type=jnp.float32
    )


def outer_cols(operand_a, operand_b):
    return lax.dot_general(
        operand_a, operand_b, (((1,), (1,)), ((), ())), preferred_element_type=jnp.float32
    )


def silu_back(grad_in, pre_act):
    sigmoid_value = jax.nn.sigmoid(pre_act)
    return grad_in * sigmoid_value * (1.0 + pre_act * (1.0 - sigmoid_value))


def geglu(value_part, gate_part):
    return value_part * jax.nn.gelu(gate_part, approximate=False)


def tap_masks(placed):
    pixels = IMG_H * IMG_W
    column = placed % IMG_W
    image_line = placed % pixels // IMG_W
    result = []
    for tap_index in range(9):
        row_step = tap_index // 3 - 1
        col_step = tap_index % 3 - 1
        inside = (
            (image_line + row_step >= 0)
            & (image_line + row_step < IMG_H)
            & (column + col_step >= 0)
            & (column + col_step < IMG_W)
        )
        result.append(inside)
    return jnp.stack(result).astype(jnp.bfloat16)


def tap_offset(tap_index):
    return (tap_index // 3 - 1) * IMG_W + tap_index % 3 - 1


def attend(query_rows, key_rows, value_rows, live_mask, score_scale):
    scores = jnp.where(live_mask, outer_cols(query_rows, key_rows) * score_scale, NEG)
    top_score = jnp.max(scores, axis=1, keepdims=True)
    log_total = top_score + jnp.log(jnp.sum(jnp.exp(scores - top_score), axis=1, keepdims=True))
    attn_probs = narrow(jnp.exp(scores - log_total))
    return (product(attn_probs, value_rows), log_total)


def attend_back(query_rows, key_rows, value_rows, live_mask, log_total, grad_rows, score_scale):
    scores = jnp.where(live_mask, outer_cols(query_rows, key_rows) * score_scale, NEG)
    attn_probs = jnp.exp(scores - log_total)
    grad_probs = outer_cols(grad_rows, value_rows)
    delta = jnp.sum(attn_probs * grad_probs, axis=1, keepdims=True)
    grad_scores = narrow(attn_probs * (grad_probs - delta))
    grad_query = product(grad_scores, key_rows) * score_scale
    grad_keys = inner_rows(grad_scores, query_rows) * score_scale
    grad_values = inner_rows(narrow(attn_probs), grad_rows)
    return (grad_query, grad_keys, grad_values)


def local(
    latents,
    time_embed,
    text_states,
    item_prompt,
    prompt_length,
    out_grad,
    resnorm_gain_a,
    resnorm_bias_a,
    conv_weight_a,
    conv_bias_a,
    time_weight,
    time_bias,
    resnorm_gain_b,
    resnorm_bias_b,
    conv_weight_b,
    conv_bias_b,
    attn_norm_gain,
    attn_norm_bias,
    qkv_weight,
    attn_out_weight,
    attn_out_bias,
    cross_norm_gain,
    cross_norm_bias,
    cross_query_weight,
    cross_kv_weight,
    cross_out_weight,
    cross_out_bias,
    geglu_norm_gain,
    geglu_norm_bias,
    geglu_in_weight,
    geglu_in_bias,
    geglu_out_weight,
    geglu_out_bias,
):
    row_count, local_chans = latents.shape
    pixels = IMG_H * IMG_W
    offset = pixels // 4
    dp_count = lax.axis_size("dp")
    dp_index = lax.axis_index("dp")
    token_total = row_count * dp_count
    item_total = token_total // pixels
    group_width = C // GROUPS
    local_groups = local_chans // group_width
    heads_local = local_chans // HEAD
    score_scale = 1.0 / math.sqrt(HEAD)
    first_row = dp_index * row_count
    placed_rows = (first_row + offset + jnp.arange(row_count, dtype=jnp.int32)) % token_total
    item_of = placed_rows // pixels
    item_match = item_of[:, None] == jnp.arange(item_total, dtype=jnp.int32)[None, :]
    item_hot = item_match.astype(jnp.float32)
    ext_rows = (
        first_row
        + offset
        + token_total
        - IMG_W
        - 1
        + jnp.arange(row_count + 2 * IMG_W + 2, dtype=jnp.int32)
    ) % token_total
    ext_masks = tap_masks(ext_rows)
    row_masks = ext_masks[:, 1 + IMG_W : 1 + IMG_W + row_count]
    slot_count = row_count // pixels + 2
    first_item = item_of[0]
    last_item = item_of[row_count - 1]
    slot_of = (item_of - first_item + item_total) % item_total
    slot_hot = (slot_of[:, None] == jnp.arange(slot_count, dtype=jnp.int32)[None, :]).astype(
        jnp.float32
    )
    head_rows = (item_of == first_item).astype(jnp.float32)
    tail_rows = (item_of == last_item).astype(jnp.float32)
    lower_share = (placed_rows[0] % pixels != 0).astype(jnp.float32)
    upper_share = ((first_row + row_count + offset) % token_total % pixels != 0).astype(jnp.float32)

    def item_means(first_term, second_term):
        stacked = (
            jnp.stack([first_term, second_term])
            .reshape(2, row_count, local_groups, group_width)
            .sum(axis=3)
        )
        slot_sums = jnp.einsum("rk,srg->skg", slot_hot, stacked, precision=HIGH)
        head_sum = jnp.einsum("r,srg->sg", head_rows, stacked, precision=HIGH)
        tail_sum = jnp.einsum("r,srg->sg", tail_rows, stacked, precision=HIGH)
        near = padded_2(jnp.stack([head_sum, tail_sum]), (("dp", 0),), 1)
        per_row = (
            jnp.einsum("rk,skg->srg", slot_hot, slot_sums, precision=HIGH)
            + (lower_share * head_rows)[None, :, None] * near[0][:, None, :]
            + (upper_share * tail_rows)[None, :, None] * near[3][:, None, :]
        ) / (pixels * group_width)
        return jnp.broadcast_to(
            per_row[..., None], (2, row_count, local_groups, group_width)
        ).reshape(2, row_count, local_chans)

    def group_forward(array_in):
        means = item_means(array_in, array_in * array_in)
        inverse = lax.rsqrt(means[1] - means[0] * means[0] + EPS)
        return ((array_in - means[0]) * inverse, inverse)

    def group_backward(grad_in, normed, inverse, gain):
        scaled = grad_in * gain
        means = item_means(scaled, scaled * normed)
        return inverse * (scaled - means[0] - normed * means[1])

    def row_means(first_term, second_term):
        sums = lax.psum(
            jnp.stack([jnp.sum(first_term, axis=1), jnp.sum(second_term, axis=1)]), "mp"
        )
        return sums[:, :, None] / C

    def layer_forward(array_in):
        means = row_means(array_in, array_in * array_in)
        inverse = lax.rsqrt(means[1] - means[0] * means[0] + EPS)
        return ((array_in - means[0]) * inverse, inverse)

    def layer_backward(grad_in, normed, inverse, gain):
        scaled = grad_in * gain
        means = row_means(scaled, scaled * normed)
        return inverse * (scaled - means[0] - normed * means[1])

    def spread(array_in):
        return lax.all_gather(array_in, "mp", axis=1, tiled=True)

    def collect(array_in):
        return lax.psum_scatter(
            array_in.astype(jnp.bfloat16), "mp", scatter_dimension=1, tiled=True
        ).astype(jnp.float32)

    def pad_rows(array_in):
        extended = padded_2(array_in, (("dp", 0),), IMG_W)
        return jnp.pad(extended, ((1, 1), (0, 0)))

    def conv_apply(padded, weight_full):
        total = jnp.zeros((row_count, weight_full.shape[2]), jnp.float32)
        for tap_index in range(9):
            start = 1 + IMG_W + tap_offset(tap_index)
            window = lax.slice_in_dim(padded, start, start + row_count, axis=0)
            total = total + row_masks[tap_index][:, None].astype(jnp.float32) * product(
                window, weight_full[tap_index]
            )
        return total

    def conv_back(padded_in, grad_low, weight_full):
        grad_ext = pad_rows(grad_low)
        input_grad = jnp.zeros((row_count, C), jnp.float32)
        weight_parts = []
        for tap_index in range(9):
            step = tap_offset(tap_index)
            masked = grad_ext * ext_masks[tap_index][:, None]
            source = lax.slice_in_dim(
                masked, 1 + IMG_W - step, 1 + IMG_W - step + row_count, axis=0
            )
            input_grad = input_grad + outer_cols(source, weight_full[tap_index])
            local_grad = lax.slice_in_dim(masked, 1 + IMG_W, 1 + IMG_W + row_count, axis=0)
            window = lax.slice_in_dim(
                padded_in, 1 + IMG_W + step, 1 + IMG_W + step + row_count, axis=0
            )
            weight_parts.append(inner_rows(window, local_grad))
        return (input_grad, jnp.stack(weight_parts))

    conv_a_full, conv_b_full, time_full = (
        lax.all_gather(conv_weight_a, "dp", axis=1, tiled=True),
        lax.all_gather(conv_weight_b, "dp", axis=1, tiled=True),
        lax.all_gather(time_weight, "dp", axis=0, tiled=True),
    )
    (
        qkv_full,
        attn_out_full,
        cross_query_full,
        cross_kv_full,
        cross_out_full,
        geglu_in_full,
        geglu_out_full,
    ) = (
        lax.all_gather(qkv_weight, "dp", axis=1, tiled=True),
        lax.all_gather(attn_out_weight, "dp", axis=1, tiled=True),
        lax.all_gather(cross_query_weight, "dp", axis=0, tiled=True),
        lax.all_gather(cross_kv_weight, "dp", axis=1, tiled=True),
        lax.all_gather(cross_out_weight, "dp", axis=1, tiled=True),
        lax.all_gather(geglu_in_weight, "dp", axis=0, tiled=True),
        lax.all_gather(geglu_out_weight, "dp", axis=1, tiled=True),
    )
    latent_in = latents.astype(jnp.float32)
    time_in = narrow(jax.nn.silu(time_embed.astype(jnp.float32)))
    time_terms = product(time_in, time_full) + time_bias
    row_terms = jnp.dot(item_hot, time_terms, precision=HIGH)
    normed_a, inverse_a = group_forward(latent_in)
    pre_a = normed_a * resnorm_gain_a + resnorm_bias_a
    padded_a = pad_rows(spread(narrow(jax.nn.silu(pre_a))))
    middle = conv_apply(padded_a, conv_a_full) + conv_bias_a + row_terms
    normed_b, inverse_b = group_forward(middle)
    pre_b = normed_b * resnorm_gain_b + resnorm_bias_b
    padded_b = pad_rows(spread(narrow(jax.nn.silu(pre_b))))
    resid = latent_in + conv_apply(padded_b, conv_b_full) + conv_bias_b
    normed_one, inverse_one = layer_forward(resid)
    full_one = spread(narrow(normed_one * attn_norm_gain + attn_norm_bias))
    qkv_rows = narrow(
        jnp.einsum("rc,kcd->krd", full_one, qkv_full, preferred_element_type=jnp.float32)
    )
    kv_ext = padded_2(qkv_rows[1:], (("dp", 1),), pixels)
    key_placed = (
        first_row
        + offset
        + token_total
        - pixels
        + jnp.arange(row_count + 2 * pixels, dtype=jnp.int32)
    ) % token_total
    live_self = item_of[:, None] == (key_placed // pixels)[None, :]
    self_outs = []
    self_lse = []
    for head_index in range(heads_local):
        cols = slice(head_index * HEAD, (head_index + 1) * HEAD)
        head_out, head_lse = attend(
            qkv_rows[0][:, cols], kv_ext[0][:, cols], kv_ext[1][:, cols], live_self, score_scale
        )
        self_outs.append(head_out)
        self_lse.append(head_lse)
    attended = narrow(jnp.concatenate(self_outs, axis=1))
    resid_two = resid + collect(product(attended, attn_out_full)) + attn_out_bias
    normed_two, inverse_two = layer_forward(resid_two)
    full_two = spread(narrow(normed_two * cross_norm_gain + cross_norm_bias))
    cross_query = narrow(product(full_two, cross_query_full))
    text_flat = text_states.reshape(PROMPTS * TXT_LEN, TXT)
    text_kv = narrow(
        jnp.einsum("pt,ktd->kpd", text_flat, cross_kv_full, preferred_element_type=jnp.float32)
    )
    key_index = jnp.arange(PROMPTS * TXT_LEN, dtype=jnp.int32)
    key_prompt = key_index // TXT_LEN
    key_length = jnp.broadcast_to(prompt_length[:, None], (PROMPTS, TXT_LEN)).reshape(
        PROMPTS * TXT_LEN
    )
    row_prompt = jnp.sum(jnp.where(item_match, item_prompt[None, :], 0), axis=1)
    live_cross = (row_prompt[:, None] == key_prompt[None, :]) & (key_index % TXT_LEN < key_length)[
        None, :
    ]
    cross_outs = []
    cross_lse = []
    for head_index in range(heads_local):
        cols = slice(head_index * HEAD, (head_index + 1) * HEAD)
        head_out, head_lse = attend(
            cross_query[:, cols], text_kv[0][:, cols], text_kv[1][:, cols], live_cross, score_scale
        )
        cross_outs.append(head_out)
        cross_lse.append(head_lse)
    cross_attended = narrow(jnp.concatenate(cross_outs, axis=1))
    resid_three = resid_two + collect(product(cross_attended, cross_out_full)) + cross_out_bias
    normed_three, inverse_three = layer_forward(resid_three)
    full_three = spread(narrow(normed_three * geglu_norm_gain + geglu_norm_bias))
    pre_ff = (
        jnp.einsum("rc,cjf->rjf", full_three, geglu_in_full, preferred_element_type=jnp.float32)
        + geglu_in_bias
    )
    hidden = narrow(geglu(pre_ff[:, 0], pre_ff[:, 1]))
    block_out = narrow(resid_three + collect(product(hidden, geglu_out_full)) + geglu_out_bias)
    (
        conv_a_back,
        conv_b_back,
        qkv_back,
        attn_out_back,
        cross_query_back,
        cross_out_back,
        geglu_in_back,
        geglu_out_back,
    ) = (
        lax.all_gather(conv_weight_a, "dp", axis=1, tiled=True),
        lax.all_gather(conv_weight_b, "dp", axis=1, tiled=True),
        lax.all_gather(qkv_weight, "dp", axis=1, tiled=True),
        lax.all_gather(attn_out_weight, "dp", axis=1, tiled=True),
        lax.all_gather(cross_query_weight, "dp", axis=0, tiled=True),
        lax.all_gather(cross_out_weight, "dp", axis=1, tiled=True),
        lax.all_gather(geglu_in_weight, "dp", axis=0, tiled=True),
        lax.all_gather(geglu_out_weight, "dp", axis=1, tiled=True),
    )
    grad_three = out_grad.astype(jnp.float32)
    geglu_out_bias_grad = jnp.sum(grad_three, axis=0)
    grad_full = spread(narrow(grad_three))
    geglu_out_weight_grad = inner_rows(hidden, grad_full)
    d_hidden = outer_cols(grad_full, geglu_out_back)
    _, geglu_pull = jax.vjp(geglu, pre_ff[:, 0], pre_ff[:, 1])
    d_value, d_gate = geglu_pull(d_hidden)
    d_pre = jnp.stack([d_value, d_gate], axis=1)
    geglu_in_bias_grad = jnp.sum(d_pre, axis=0)
    d_pre_low = narrow(d_pre)
    geglu_in_weight_grad = jnp.einsum(
        "rc,rjf->cjf", full_three, d_pre_low, preferred_element_type=jnp.float32
    )
    d_norm_three = collect(
        jnp.einsum("rjf,cjf->rc", d_pre_low, geglu_in_back, preferred_element_type=jnp.float32)
    )
    geglu_norm_gain_grad = jnp.sum(d_norm_three * normed_three, axis=0)
    geglu_norm_bias_grad = jnp.sum(d_norm_three, axis=0)
    grad_two = grad_three + layer_backward(
        d_norm_three, normed_three, inverse_three, geglu_norm_gain
    )
    cross_out_bias_grad = jnp.sum(grad_two, axis=0)
    cross_full = spread(narrow(grad_two))
    cross_out_weight_grad = inner_rows(cross_attended, cross_full)
    d_cross = narrow(outer_cols(cross_full, cross_out_back))
    cross_query_parts = []
    text_key_parts = []
    text_value_parts = []
    for head_index in range(heads_local):
        cols = slice(head_index * HEAD, (head_index + 1) * HEAD)
        grad_query, grad_keys, grad_values = attend_back(
            cross_query[:, cols],
            text_kv[0][:, cols],
            text_kv[1][:, cols],
            live_cross,
            cross_lse[head_index],
            d_cross[:, cols],
            score_scale,
        )
        cross_query_parts.append(grad_query)
        text_key_parts.append(grad_keys)
        text_value_parts.append(grad_values)
    d_cross_query = narrow(jnp.concatenate(cross_query_parts, axis=1))
    text_grad_part = jnp.stack(
        [jnp.concatenate(text_key_parts, axis=1), jnp.concatenate(text_value_parts, axis=1)]
    )
    cross_query_weight_grad = inner_rows(full_two, d_cross_query)
    d_norm_two = collect(outer_cols(d_cross_query, cross_query_back))
    cross_norm_gain_grad = jnp.sum(d_norm_two * normed_two, axis=0)
    cross_norm_bias_grad = jnp.sum(d_norm_two, axis=0)
    grad_one = grad_two + layer_backward(d_norm_two, normed_two, inverse_two, cross_norm_gain)
    attn_out_bias_grad = jnp.sum(grad_one, axis=0)
    attn_full = spread(narrow(grad_one))
    attn_out_weight_grad = inner_rows(attended, attn_full)
    d_attended = narrow(outer_cols(attn_full, attn_out_back))
    query_parts = []
    key_parts = []
    value_parts = []
    for head_index in range(heads_local):
        cols = slice(head_index * HEAD, (head_index + 1) * HEAD)
        grad_query, grad_keys, grad_values = attend_back(
            qkv_rows[0][:, cols],
            kv_ext[0][:, cols],
            kv_ext[1][:, cols],
            live_self,
            self_lse[head_index],
            d_attended[:, cols],
            score_scale,
        )
        query_parts.append(grad_query)
        key_parts.append(grad_keys)
        value_parts.append(grad_values)
    kv_grad_ext = jnp.stack(
        [jnp.concatenate(key_parts, axis=1), jnp.concatenate(value_parts, axis=1)]
    )
    edges = jnp.concatenate([kv_grad_ext[:, :pixels], kv_grad_ext[:, row_count + pixels :]], axis=1)
    returned = padded_2(edges.astype(jnp.bfloat16), (("dp", 1),), pixels).astype(edges.dtype)
    kv_grad = (
        kv_grad_ext[:, pixels : pixels + row_count]
        + jnp.pad(returned[:, :pixels], ((0, 0), (0, row_count - pixels), (0, 0)))
        + jnp.pad(returned[:, 3 * pixels :], ((0, 0), (row_count - pixels, 0), (0, 0)))
    )
    d_qkv = narrow(jnp.concatenate([jnp.concatenate(query_parts, axis=1)[None], kv_grad], axis=0))
    qkv_weight_grad = jnp.einsum("rc,krd->kcd", full_one, d_qkv, preferred_element_type=jnp.float32)
    d_norm_one = collect(
        jnp.einsum("krd,kcd->rc", d_qkv, qkv_back, preferred_element_type=jnp.float32)
    )
    attn_norm_gain_grad = jnp.sum(d_norm_one * normed_one, axis=0)
    attn_norm_bias_grad = jnp.sum(d_norm_one, axis=0)
    grad_zero = grad_one + layer_backward(d_norm_one, normed_one, inverse_one, attn_norm_gain)
    conv_bias_b_grad = jnp.sum(grad_zero, axis=0)
    d_act_b_part, conv_weight_b_part = conv_back(padded_b, narrow(grad_zero), conv_b_back)
    d_pre_b = silu_back(collect(d_act_b_part), pre_b)
    resnorm_gain_b_grad = jnp.sum(d_pre_b * normed_b, axis=0)
    resnorm_bias_b_grad = jnp.sum(d_pre_b, axis=0)
    d_middle = group_backward(d_pre_b, normed_b, inverse_b, resnorm_gain_b)
    conv_bias_a_grad = jnp.sum(d_middle, axis=0)
    time_grad_part = jnp.einsum("ri,rc->ic", item_hot, d_middle, precision=HIGH)
    d_act_a_part, conv_weight_a_part = conv_back(padded_a, narrow(d_middle), conv_a_back)
    d_pre_a = silu_back(collect(d_act_a_part), pre_a)
    resnorm_gain_a_grad = jnp.sum(d_pre_a * normed_a, axis=0)
    resnorm_bias_a_grad = jnp.sum(d_pre_a, axis=0)
    latents_grad = grad_zero + group_backward(d_pre_a, normed_a, inverse_a, resnorm_gain_a)
    vector_grads = jnp.stack(
        [
            resnorm_gain_a_grad,
            resnorm_bias_a_grad,
            conv_bias_a_grad,
            resnorm_gain_b_grad,
            resnorm_bias_b_grad,
            conv_bias_b_grad,
            attn_norm_gain_grad,
            attn_norm_bias_grad,
            attn_out_bias_grad,
            cross_norm_gain_grad,
            cross_norm_bias_grad,
            cross_out_bias_grad,
            geglu_norm_gain_grad,
            geglu_norm_bias_grad,
            geglu_out_bias_grad,
        ]
    )
    summed_vectors, summed_in_bias, summed_time, summed_text = (
        lax.psum(vector_grads.astype(jnp.bfloat16), "dp").astype(jnp.float32),
        lax.psum(geglu_in_bias_grad.astype(jnp.bfloat16), "dp").astype(jnp.float32),
        lax.psum(time_grad_part.astype(jnp.bfloat16), "dp").astype(jnp.float32),
        lax.psum(text_grad_part.astype(jnp.bfloat16), "dp").astype(jnp.float32),
    )
    temb_local = TEMB // dp_count
    time_slice = lax.dynamic_slice_in_dim(time_in, dp_index * temb_local, temb_local, axis=1)
    time_weight_grad = inner_rows(time_slice, narrow(summed_time))
    time_bias_grad = jnp.sum(summed_time, axis=0)
    text_local = TXT // dp_count
    text_slice = lax.dynamic_slice_in_dim(text_flat, dp_index * text_local, text_local, axis=1)
    text_rounded = narrow(summed_text)
    cross_kv_weight_grad = jnp.stack(
        [inner_rows(text_slice, text_rounded[0]), inner_rows(text_slice, text_rounded[1])]
    )
    (
        conv_weight_a_grad,
        conv_weight_b_grad,
        qkv_weight_out,
        attn_out_weight_out,
        cross_query_weight_out,
        cross_out_weight_out,
        geglu_in_weight_out,
        geglu_out_weight_out,
    ) = (
        lax.psum_scatter(
            conv_weight_a_part.astype(jnp.bfloat16), "dp", scatter_dimension=1, tiled=True
        ).astype(jnp.float32),
        lax.psum_scatter(
            conv_weight_b_part.astype(jnp.bfloat16), "dp", scatter_dimension=1, tiled=True
        ).astype(jnp.float32),
        lax.psum_scatter(
            qkv_weight_grad.astype(jnp.bfloat16), "dp", scatter_dimension=1, tiled=True
        ).astype(jnp.float32),
        lax.psum_scatter(
            attn_out_weight_grad.astype(jnp.bfloat16), "dp", scatter_dimension=1, tiled=True
        ).astype(jnp.float32),
        lax.psum_scatter(
            cross_query_weight_grad.astype(jnp.bfloat16), "dp", scatter_dimension=0, tiled=True
        ).astype(jnp.float32),
        lax.psum_scatter(
            cross_out_weight_grad.astype(jnp.bfloat16), "dp", scatter_dimension=1, tiled=True
        ).astype(jnp.float32),
        lax.psum_scatter(
            geglu_in_weight_grad.astype(jnp.bfloat16), "dp", scatter_dimension=0, tiled=True
        ).astype(jnp.float32),
        lax.psum_scatter(
            geglu_out_weight_grad.astype(jnp.bfloat16), "dp", scatter_dimension=1, tiled=True
        ).astype(jnp.float32),
    )
    return (
        block_out,
        latents_grad,
        summed_vectors[0],
        summed_vectors[1],
        conv_weight_a_grad,
        summed_vectors[2],
        time_weight_grad,
        time_bias_grad,
        summed_vectors[3],
        summed_vectors[4],
        conv_weight_b_grad,
        summed_vectors[5],
        summed_vectors[6],
        summed_vectors[7],
        qkv_weight_out,
        attn_out_weight_out,
        summed_vectors[8],
        summed_vectors[9],
        summed_vectors[10],
        cross_query_weight_out,
        cross_kv_weight_grad,
        cross_out_weight_out,
        summed_vectors[11],
        summed_vectors[12],
        summed_vectors[13],
        geglu_in_weight_out,
        summed_in_bias,
        geglu_out_weight_out,
        summed_vectors[14],
    )


def solution(mesh):
    return jax.shard_map(
        local,
        mesh=mesh,
        in_specs=(
            P("dp", "mp"),
            P(),
            P(),
            P(),
            P(),
            P("dp", "mp"),
            P("mp"),
            P("mp"),
            P(None, "dp", "mp"),
            P("mp"),
            P("dp", "mp"),
            P("mp"),
            P("mp"),
            P("mp"),
            P(None, "dp", "mp"),
            P("mp"),
            P("mp"),
            P("mp"),
            P(None, "dp", "mp"),
            P("mp", "dp"),
            P("mp"),
            P("mp"),
            P("mp"),
            P("dp", "mp"),
            P(None, "dp", "mp"),
            P("mp", "dp"),
            P("mp"),
            P("mp"),
            P("mp"),
            P("dp", None, "mp"),
            P(None, "mp"),
            P("mp", "dp"),
            P("mp"),
        ),
        out_specs=(
            P("dp", "mp"),
            P("dp", "mp"),
            P("mp"),
            P("mp"),
            P(None, "dp", "mp"),
            P("mp"),
            P("dp", "mp"),
            P("mp"),
            P("mp"),
            P("mp"),
            P(None, "dp", "mp"),
            P("mp"),
            P("mp"),
            P("mp"),
            P(None, "dp", "mp"),
            P("mp", "dp"),
            P("mp"),
            P("mp"),
            P("mp"),
            P("dp", "mp"),
            P(None, "dp", "mp"),
            P("mp", "dp"),
            P("mp"),
            P("mp"),
            P("mp"),
            P("dp", None, "mp"),
            P(None, "mp"),
            P("mp", "dp"),
            P("mp"),
        ),
        check_vma=False,
    )
```

profile of v0, /device:TPU:0, one launch (start us, length us, event | category | flops | bytes accessed | tf_op | source)
XLA Modules:
  0.0 2075.2 jit_solution(16167647415882904402)
XLA Ops:
  27.1 32.6 %all_gather.64 = bf16[1280,320]{1,0:T(8,128)(2,1)S(1)} all-gather(bf16[160,320]{1,0:T(8,128)(2,1)S(1)} %copy-done.130), channel_id=1, replica_groups=mesh['dp'=8,'mp'=4] {'dp'}, dimensions={0}, use_global_device_ids=true | all-gather | bytes 921600 | tf_op jit(solution)/shard_map/all_gather | solution.py:269
  69.7 14.0 collective-permute-done.3
  87.1 96.6 %all-gather.17.cloned.1.call-done = bf16[9,1280,320]{2,1,0:T(8,128)(2,1)} async-done(((bf16[9,160,320]{2,1,0:T(8,128)(2,1)}), bf16[9,1280,320]{2,1,0:T(8,128)(2,1)}) %all-gather.17.cloned.1.call-update) | async-done | bytes 7372816 | tf_op jit(solution)/shard_map/all_gather | solution.py:267
  212.3 20.4 all-gather.19.cloned.1.call-done
  238.7 126.9 %all-gather.21.cloned.1.call-done = bf16[9,1280,320]{2,1,0:T(8,128)(2,1)} async-done(((bf16[9,160,320]{2,1,0:T(8,128)(2,1)}), bf16[9,1280,320]{2,1,0:T(8,128)(2,1)}) %all-gather.21.cloned.1.call-update) | async-done | bytes 7372816 | tf_op jit(solution)/shard_map/all_gather | solution.py:268
  382.8 6.8 psum.70
  390.7 36.8 %all_gather.69 = bf16[320,1280]{0,1:T(8,128)(2,1)} all-gather(bf16[320,160]{0,1:T(8,128)(2,1)S(1)} %copy-done.131), channel_id=1, replica_groups=mesh['dp'=8,'mp'=4] {'dp'}, dimensions={1}, use_global_device_ids=true | all-gather | bytes 921600 | tf_op jit(solution)/shard_map/all_gather | solution.py:281
  427.5 11.8 all-gather.25.cloned.1.call-done
  439.3 20.8 %all-gather.23.cloned.1.call-done = bf16[640,1280]{0,1:T(8,128)(2,1)} async-done(((bf16[640,320]{0,1:T(8,128)(2,1)}), bf16[640,1280]{0,1:T(8,128)(2,1)}) %all-gather.23.cloned.1.call-update) | async-done | bytes 1638416 | tf_op jit(solution)/shard_map/all_gather | solution.py:227
  469.5 11.0 collective-permute-done.8
  496.7 26.7 %reduce-scatter.23.cloned.1.call-done = bf16[640,320]{0,1:T(8,128)(2,1)} async-done(((bf16[640,1280]{0,1:T(8,128)(2,1)}), bf16[640,320]{0,1:T(8,128)(2,1)}) %reduce-scatter.23.cloned.1.call-update) | async-done | bytes 409616 | tf_op jit(solution)/shard_map/reduce_scatter | solution.py:230
  525.8 5.9 psum.71
  543.3 37.4 %all_gather.71 = bf16[1280,320]{1,0:T(8,128)(2,1)} all-gather(bf16[160,320]{1,0:T(8,128)(2,1)S(1)} %copy-done.132), channel_id=1, replica_groups=mesh['dp'=8,'mp'=4] {'dp'}, dimensions={0}, use_global_device_ids=true | all-gather | bytes 921600 | tf_op jit(solution)/shard_map/all_gather | solution.py:282
  580.7 36.2 %all_gather.73 = bf16[320,1280]{0,1:T(8,128)(2,1)} all-gather(bf16[320,160]{0,1:T(8,128)(2,1)S(1)} %copy-done.133), channel_id=1, replica_groups=mesh['dp'=8,'mp'=4] {'dp'}, dimensions={1}, use_global_device_ids=true | all-gather | bytes 921600 | tf_op jit(solution)/shard_map/all_gather | solution.py:284
  638.2 25.5 %reduce-scatter.25.cloned.1.call-done = bf16[640,320]{0,1:T(8,128)(2,1)} async-done(((bf16[640,1280]{0,1:T(8,128)(2,1)}), bf16[640,320]{0,1:T(8,128)(2,1)}) %reduce-scatter.25.cloned.1.call-update) | async-done | bytes 409616 | tf_op jit(solution)/shard_map/reduce_scatter | solution.py:230
  674.3 11.2 all-gather.37.cloned.1.call-done
  685.4 64.1 %all-gather.35.cloned.1.call-done = bf16[1280,1280]{0,1:T(8,128)(2,1)} async-done(((bf16[1280,160]{0,1:T(8,128)(2,1)}), bf16[1280,1280]{0,1:T(8,128)(2,1)}) %all-gather.35.cloned.1.call-update) | async-done | bytes 3276816 | tf_op jit(solution)/shard_map/all_gather | solution.py:286
  749.5 6.5 fusion.562
  755.9 97.2 %all-gather.33.cloned.1.call-done = bf16[1280,2,1280]{2,0,1:T(8,128)(2,1)} async-done(((bf16[160,2,1280]{2,0,1:T(8,128)(2,1)}), bf16[1280,2,1280]{2,0,1:T(8,128)(2,1)}) %all-gather.33.cloned.1.call-update) | async-done | bytes 6553616 | tf_op jit(solution)/shard_map/all_gather | solution.py:285
  853.1 20.2 all-gather.31.cloned.1.call-done
  873.3 7.3 convolution_add_fusion
  880.7 7.1 multiply_bitcast_fusion
  892.1 6.4 fusion.27
  898.6 6.3 convolution_convert_fusion.6
  905.2 22.1 %reduce-scatter.29.cloned.1.call-done = bf16[640,320]{0,1:T(8,128)(2,1)} async-done(((bf16[640,1280]{0,1:T(8,128)(2,1)}), bf16[640,320]{0,1:T(8,128)(2,1)}) %reduce-scatter.29.cloned.1.call-update) | async-done | bytes 409616 | tf_op jit(solution)/shard_map/reduce_scatter | solution.py:230
  935.4 23.1 %reduce-scatter.27.cloned.1.call-done = bf16[640,320]{0,1:T(8,128)(2,1)} async-done(((bf16[640,1280]{0,1:T(8,128)(2,1)}), bf16[640,320]{0,1:T(8,128)(2,1)}) %reduce-scatter.27.cloned.1.call-update) | async-done | bytes 409616 | tf_op jit(solution)/shard_map/reduce_scatter | solution.py:230
  963.5 20.1 all-gather.39.cloned.1.call-done
  997.1 28.7 %reduce-scatter.31.cloned.1.call-done = bf16[640,320]{0,1:T(8,128)(2,1)} async-done(((bf16[640,1280]{0,1:T(8,128)(2,1)}), bf16[640,320]{0,1:T(8,128)(2,1)}) %reduce-scatter.31.cloned.1.call-update) | async-done | bytes 409616 | tf_op jit(solution)/shard_map/reduce_scatter | solution.py:230
  1028.0 5.9 psum.74
  1038.6 20.8 %all-gather.41.cloned.1.call-done = bf16[640,1280]{0,1:T(8,128)(2,1)} async-done(((bf16[640,320]{0,1:T(8,128)(2,1)}), bf16[640,1280]{0,1:T(8,128)(2,1)}) %all-gather.41.cloned.1.call-update) | async-done | bytes 1638416 | tf_op jit(solution)/shard_map/all_gather | solution.py:227
  1086.5 9.9 collective-permute-done.10
  1104.7 27.5 %reduce-scatter.33.cloned.1.call-done = bf16[640,320]{0,1:T(8,128)(2,1)} async-done(((bf16[640,1280]{0,1:T(8,128)(2,1)}), bf16[640,320]{0,1:T(8,128)(2,1)}) %reduce-scatter.33.cloned.1.call-update) | async-done | bytes 409616 | tf_op jit(solution)/shard_map/reduce_scatter | solution.py:230
  1194.1 9.3 convolution_convert_fusion
  1208.2 6.2 copy.97
  1214.4 8.3 reshape.847
  1278.3 20.1 copy.95
  1298.4 18.9 reshape.845
  1342.2 20.4 copy.93
  1362.5 18.8 reshape.843
  1396.0 25.7 %reduce-scatter.43.cloned.1.call-done = bf16[320,160]{0,1:T(8,128)(2,1)} async-done(((bf16[320,1280]{0,1:T(8,128)(2,1)}), bf16[320,160]{0,1:T(8,128)(2,1)}) %reduce-scatter.43.cloned.1.call-update) | async-done | bytes 102416 | tf_op jit(solution)/shard_map/reduce_scatter | solution.py:542
  1423.3 64.5 %reduce-scatter.41.cloned.1.call-done = bf16[160,320]{1,0:T(8,128)(2,1)} async-done(((bf16[1280,320]{1,0:T(8,128)(2,1)}), bf16[160,320]{1,0:T(8,128)(2,1)}) %reduce-scatter.41.cloned.1.call-update) | async-done | bytes 102416 | tf_op jit(solution)/shard_map/reduce_scatter | solution.py:539
  1489.6 64.4 %reduce-scatter.39.cloned.1.call-done = bf16[320,160]{0,1:T(8,128)(2,1)} async-done(((bf16[320,1280]{0,1:T(8,128)(2,1)}), bf16[320,160]{0,1:T(8,128)(2,1)}) %reduce-scatter.39.cloned.1.call-update) | async-done | bytes 102416 | tf_op jit(solution)/shard_map/reduce_scatter | solution.py:536
  1555.5 123.0 %reduce-scatter.45.cloned.1.call-done = bf16[160,2,1280]{2,0,1:T(8,128)(2,1)} async-done(((bf16[1280,2,1280]{2,0,1:T(8,128)(2,1)}), bf16[160,2,1280]{2,0,1:T(8,128)(2,1)}) %reduce-scatter.45.cloned.1.call-update) | async-done | bytes 819216 | tf_op jit(solution)/shard_map/reduce_scatter | solution.py:545
  1681.9 69.6 %reduce-scatter.53.cloned.1.call-done = bf16[160,960]{1,0:T(8,128)(2,1)} async-done(((bf16[1280,960]{1,0:T(8,128)(2,1)}), bf16[160,960]{1,0:T(8,128)(2,1)}) %reduce-scatter.53.cloned.1.call-update) | async-done | bytes 307216
  1755.2 26.4 %reduce-scatter.37.cloned.1.call-done = bf16[640,320]{0,1:T(8,128)(2,1)} async-done(((bf16[640,1280]{0,1:T(8,128)(2,1)}), bf16[640,320]{0,1:T(8,128)(2,1)}) %reduce-scatter.37.cloned.1.call-update) | async-done | bytes 409616 | tf_op jit(solution)/shard_map/reduce_scatter | solution.py:230
  1788.4 40.8 %all-reduce.5 = (bf16[15,320]{1,0:T(8,128)(2,1)S(1)}, bf16[20,320]{1,0:T(8,128)(2,1)S(1)}, bf16[2,1280]{1,0:T(2,128)(2,1)S(1)}) all-reduce(bf16[15,320]{1,0:T(8,128)(2,1)S(1)} %stack.369, bf16[20,320]{1,0:T(8,128)(2,1)S(1)} %convolution_convert_fusion.47, bf16[2,1280]{1,0:T(2,128)(2,1)S(1)} %fusion), channel_id=1, replica_groups=mesh['dp'=8,'mp'=4] {'dp'}, use_global_device_ids=true, to_apply=%region_76.77 | all-reduce | flops 13760 | bytes 55040 | tf_op jit(solution)/shard_map/psum | solution.py:502
  1833.8 89.6 %reduce-scatter.51.cloned.1.call-done = bf16[160,2880]{1,0:T(8,128)(2,1)} async-done(((bf16[1280,2880]{1,0:T(8,128)(2,1)}), bf16[160,2880]{1,0:T(8,128)(2,1)}) %reduce-scatter.51.cloned.1.call-update) | async-done | bytes 921616
  1929.6 132.4 %reduce-scatter.49.cloned.1.call-done = bf16[160,2880]{1,0:T(8,128)(2,1)} async-done(((bf16[1280,2880]{1,0:T(8,128)(2,1)}), bf16[160,2880]{1,0:T(8,128)(2,1)}) %reduce-scatter.49.cloned.1.call-update) | async-done | bytes 921616
  (849 shorter events, 422.5 us)
Async XLA Ops:
  7.2 53.4 %all-gather.15.cloned.1.call-start = ((), (), s32[]{:S(2)}) async-start(), calls=%async_computation.16 | async-start | bytes 2048000 | tf_op jit(solution)/shard_map/all_gather | solution.py:227
  11.8 11.3 collective-permute-start
  15.1 8.0 collective-permute-start.1
  25.1 158.7 %all-gather.17.cloned.1.call-start = ((), (), s32[]{:S(2)}) async-start(), calls=%async_computation.17 | async-start | bytes 9953280 | tf_op jit(solution)/shard_map/all_gather | solution.py:267
  25.8 206.9 %all-gather.19.cloned.1.call-start = ((), (), s32[]{:S(2)}) async-start(), calls=%async_computation.18 | async-start | bytes 2048000 | tf_op jit(solution)/shard_map/all_gather | solution.py:227
  62.0 22.5 %collective-permute-start.2 = (bf16[16,1280]{0,1:T(8,128)(2,1)S(1)}, bf16[16,1280]{0,1:T(8,128)(2,1)S(1)}, u32[]{:S(2)}, u32[]{:S(2)}) collective-permute-start(bf16[16,1280]{0,1:T(8,128)(2,1)S(1)} %get-tuple-element.240), channel_id=1, source_target_pairs={{0,4},{4,8},{8,12},{12,16},{16,20},{20,24},{24,28},{28,0},{1,5},{5... | collective-permute-start | bytes 122888 | tf_op jit(solution)/shard_map/ppermute | solution.py:31
  62.1 21.6 %collective-permute-start.3 = (bf16[16,1280]{0,1:T(8,128)(2,1)S(1)}, bf16[16,1280]{0,1:T(8,128)(2,1)S(1)}, u32[]{:S(2)}, u32[]{:S(2)}) collective-permute-start(bf16[16,1280]{0,1:T(8,128)(2,1)S(1)} %get-tuple-element.241), channel_id=1, source_target_pairs={{4,0},{8,4},{12,8},{16,12},{20,16},{24,20},{28,24},{0,28},{5,1},{9... | collective-permute-start | bytes 122888 | tf_op jit(solution)/shard_map/ppermute | solution.py:32
  203.1 6.3 collective-permute-start.4
  211.1 154.5 %all-gather.21.cloned.1.call-start = ((), (), s32[]{:S(2)}) async-start(), calls=%async_computation.19 | async-start | bytes 9953280 | tf_op jit(solution)/shard_map/all_gather | solution.py:268
  211.7 227.6 %all-gather.25.cloned.1.call-start = ((), (), s32[]{:S(2)}) async-start(), calls=%async_computation.21 | async-start | bytes 3317760 | tf_op jit(solution)/shard_map/all_gather | solution.py:280
  212.3 247.8 %all-gather.23.cloned.1.call-start = ((), (), s32[]{:S(2)}) async-start(), calls=%async_computation.20 | async-start | bytes 2048000 | tf_op jit(solution)/shard_map/all_gather | solution.py:227
  233.9 134.6 %collective-permute-start.6 = (bf16[16,1280]{0,1:T(8,128)(2,1)S(1)}, bf16[16,1280]{0,1:T(8,128)(2,1)S(1)}, u32[]{:S(2)}, u32[]{:S(2)}) collective-permute-start(bf16[16,1280]{0,1:T(8,128)(2,1)S(1)} %get-tuple-element.238), channel_id=1, source_target_pairs={{0,4},{4,8},{8,12},{12,16},{16,20},{20,24},{24,28},{28,0},{1,5},{5... | collective-permute-start | bytes 122888 | tf_op jit(solution)/shard_map/ppermute | solution.py:31
  235.5 132.9 %collective-permute-start.7 = (bf16[16,1280]{0,1:T(8,128)(2,1)S(1)}, bf16[16,1280]{0,1:T(8,128)(2,1)S(1)}, u32[]{:S(2)}, u32[]{:S(2)}) collective-permute-start(bf16[16,1280]{0,1:T(8,128)(2,1)S(1)} %get-tuple-element.239), channel_id=1, source_target_pairs={{4,0},{8,4},{12,8},{16,12},{20,16},{24,20},{28,24},{0,28},{5,1},{9... | collective-permute-start | bytes 122888 | tf_op jit(solution)/shard_map/ppermute | solution.py:32
  390.7 132.8 %reduce-scatter.23.cloned.1.call-start = ((), (), s32[]{:S(2)}) async-start(), calls=%async_computation.22 | async-start | bytes 2048000 | tf_op jit(solution)/shard_map/reduce_scatter | solution.py:230
  464.6 15.9 collective-permute-start.8
  466.1 16.6 collective-permute-start.9
  495.9 121.1 %all-gather.29.cloned.1.call-start = ((), (), s32[]{:S(2)}) async-start(), calls=%async_computation.24 | async-start | bytes 2949120 | tf_op jit(solution)/shard_map/all_gather | solution.py:283
  496.7 125.9 %all-gather.27.cloned.1.call-start = ((), (), s32[]{:S(2)}) async-start(), calls=%async_computation.23 | async-start | bytes 2048000 | tf_op jit(solution)/shard_map/all_gather | solution.py:227
  533.9 129.9 %reduce-scatter.25.cloned.1.call-start = ((), (), s32[]{:S(2)}) async-start(), calls=%async_computation.25 | async-start | bytes 2048000 | tf_op jit(solution)/shard_map/reduce_scatter | solution.py:230
  634.7 50.8 %all-gather.37.cloned.1.call-start = ((), (), s32[]{:S(2)}) async-start(), calls=%async_computation.30 | async-start | bytes 2048000 | tf_op jit(solution)/shard_map/all_gather | solution.py:227
  635.4 114.1 %all-gather.35.cloned.1.call-start = ((), (), s32[]{:S(2)}) async-start(), calls=%async_computation.28 | async-start | bytes 3686400 | tf_op jit(solution)/shard_map/all_gather | solution.py:286
  636.0 217.1 %all-gather.33.cloned.1.call-start = ((), (), s32[]{:S(2)}) async-start(), calls=%async_computation.27 | async-start | bytes 7372800 | tf_op jit(solution)/shard_map/all_gather | solution.py:285
  638.2 235.1 %all-gather.31.cloned.1.call-start = ((), (), s32[]{:S(2)}) async-start(), calls=%async_computation.26 | async-start | bytes 2048000 | tf_op jit(solution)/shard_map/all_gather | solution.py:227
  674.2 253.1 %reduce-scatter.29.cloned.1.call-start = ((), (), s32[]{:S(2)}) async-start(), calls=%async_computation.31 | async-start | bytes 2048000 | tf_op jit(solution)/shard_map/reduce_scatter | solution.py:230
  898.5 60.0 %reduce-scatter.27.cloned.1.call-start = ((), (), s32[]{:S(2)}) async-start(), calls=%async_computation.29 | async-start | bytes 2048000 | tf_op jit(solution)/shard_map/reduce_scatter | solution.py:230
  904.9 78.6 %all-gather.39.cloned.1.call-start = ((), (), s32[]{:S(2)}) async-start(), calls=%async_computation.32 | async-start | bytes 2048000 | tf_op jit(solution)/shard_map/all_gather | solution.py:227
  963.4 62.4 %reduce-scatter.31.cloned.1.call-start = ((), (), s32[]{:S(2)}) async-start(), calls=%async_computation.33 | async-start | bytes 2048000 | tf_op jit(solution)/shard_map/reduce_scatter | solution.py:230
  997.0 62.4 %all-gather.41.cloned.1.call-start = ((), (), s32[]{:S(2)}) async-start(), calls=%async_computation.34 | async-start | bytes 2048000 | tf_op jit(solution)/shard_map/all_gather | solution.py:227
  1038.1 94.0 %reduce-scatter.33.cloned.1.call-start = ((), (), s32[]{:S(2)}) async-start(), calls=%async_computation.35 | async-start | bytes 2048000 | tf_op jit(solution)/shard_map/reduce_scatter | solution.py:230
  1080.5 15.9 collective-permute-start.10
  1082.0 16.6 collective-permute-start.11
  1104.6 118.4 %reduce-scatter.35.cloned.1.call-start = ((), (), s32[]{:S(2)}) async-start(), calls=%async_computation.36 | async-start | bytes 2048000 | tf_op jit(solution)/shard_map/reduce_scatter | solution.py:230
  1142.1 7.2 collective-permute-start.12
  1166.9 223.3 %all-reduce.8.cloned.1.call-start = ((), (), s32[]{:S(2)}) async-start(), calls=%async_computation.40 | async-start | bytes 1638400 | tf_op jit(solution)/shard_map/psum | solution.py:505
  1178.5 215.4 %reduce-scatter.47.cloned.1.call-start = ((), (), s32[]{:S(2)}) async-start(), calls=%async_computation.43 | async-start | bytes 3686400 | tf_op jit(solution)/shard_map/reduce_scatter | solution.py:548
  1183.5 238.2 %reduce-scatter.43.cloned.1.call-start = ((), (), s32[]{:S(2)}) async-start(), calls=%async_computation.41 | async-start | bytes 1105920 | tf_op jit(solution)/shard_map/reduce_scatter | solution.py:542
  1188.0 299.7 %reduce-scatter.41.cloned.1.call-start = ((), (), s32[]{:S(2)}) async-start(), calls=%async_computation.39 | async-start | bytes 1105920 | tf_op jit(solution)/shard_map/reduce_scatter | solution.py:539
  1190.2 363.7 %reduce-scatter.39.cloned.1.call-start = ((), (), s32[]{:S(2)}) async-start(), calls=%async_computation.38 | async-start | bytes 1105920 | tf_op jit(solution)/shard_map/reduce_scatter | solution.py:536
  1194.1 484.5 %reduce-scatter.45.cloned.1.call-start = ((), (), s32[]{:S(2)}) async-start(), calls=%async_computation.42 | async-start | bytes 7372800 | tf_op jit(solution)/shard_map/reduce_scatter | solution.py:545
  1203.4 548.1 %reduce-scatter.53.cloned.1.call-start = ((), (), s32[]{:S(2)}) async-start(), calls=%async_computation.46 | async-start | bytes 2949120
  1222.7 558.9 %reduce-scatter.37.cloned.1.call-start = ((), (), s32[]{:S(2)}) async-start(), calls=%async_computation.37 | async-start | bytes 2048000 | tf_op jit(solution)/shard_map/reduce_scatter | solution.py:230
  1227.0 6.3 collective-permute-start.14
  1234.8 7.2 collective-permute-start.16
  1234.9 7.1 collective-permute-start.17
  1258.9 664.5 %reduce-scatter.51.cloned.1.call-start = ((), (), s32[]{:S(2)}) async-start(), calls=%async_computation.45 | async-start | bytes 8478720
  1317.3 744.7 %reduce-scatter.49.cloned.1.call-start = ((), (), s32[]{:S(2)}) async-start(), calls=%async_computation.44 | async-start | bytes 8478720
  1783.8 48.6 %collective-permute-start.19 = (f32[1,2,8]{2,1,0:T(2,128)S(1)}, f32[1,2,8]{2,1,0:T(2,128)S(1)}, u32[]{:S(2)}, u32[]{:S(2)}) collective-permute-start(f32[1,2,8]{2,1,0:T(2,128)S(1)} %bitcast.576), channel_id=1, source_target_pairs={{4,0},{8,4},{12,8},{16,12},{20,16},{24,20},{28,24},{0,28},{5,1},{9... | collective-permute-start | bytes 200 | tf_op jit(solution)/shard_map/ppermute | solution.py:32
  1788.3 44.1 %collective-permute-start.18 = (f32[1,2,8]{2,1,0:T(2,128)S(1)}, f32[1,2,8]{2,1,0:T(2,128)S(1)}, u32[]{:S(2)}, u32[]{:S(2)}) collective-permute-start(f32[1,2,8]{2,1,0:T(2,128)S(1)} %bitcast.577), channel_id=1, source_target_pairs={{0,4},{4,8},{8,12},{12,16},{16,20},{20,24},{24,28},{28,0},{1,5},{5... | collective-permute-start | bytes 200 | tf_op jit(solution)/shard_map/ppermute | solution.py:31
  (200 other events, 4918.0 us)
Sparse Core Ops, SparseCore 0:
  25.2 18.7 all-gather.14
  46.2 137.5 all-gather.16
  211.3 21.3 all-gather.18
  234.7 130.8 all-gather.20
  367.7 71.5 all-gather.24
  441.3 18.7 all-gather.22
  496.0 27.3 reduce-scatter.22
  525.7 73.4 all-gather.28
  601.4 19.7 all-gather.26
  634.8 28.9 reduce-scatter.24
  665.4 20.0 all-gather.36
  687.5 61.9 all-gather.34
  752.3 100.8 all-gather.32
  855.1 18.1 all-gather.30
  898.7 28.5 reduce-scatter.28
  929.9 28.5 reduce-scatter.26
  963.5 20.0 all-gather.38
  997.2 28.5 reduce-scatter.30
  1038.2 21.1 all-gather.40
  1104.7 27.3 reduce-scatter.32
  1167.0 29.6 reduce-scatter.34
  1201.2 75.3 all-reduce.7
  1280.6 75.4 reduce-scatter.46
  1359.3 62.3 reduce-scatter.42
  1425.4 62.3 reduce-scatter.40
  1491.5 62.3 reduce-scatter.38
  1557.8 120.7 reduce-scatter.44
  1682.1 69.3 reduce-scatter.52
  1754.1 27.4 reduce-scatter.36
  1785.5 137.8 reduce-scatter.50
  1927.0 134.9 reduce-scatter.48
where the time goes:
time: 2080 us
  waiting for transfers between devices  1310 us (63%)
  matrix products  234 us (11%)
  blocking collectives  220 us (11%)
  local copies, waits for them, and re-layouts  157 us (8%)
  other arithmetic  80.3 us (4%)
  starting transfers between devices  52.5 us (3%)
    unnamed x34, waiting for transfers between devices  295 us
    reduce_scatter x8, waiting for transfers between devices, collect(): lax.psum_scatter(array_in.astype(jnp.bfloat16), 'mp', scatter_dimension=1...  180 us
    unnamed x414, local copies, waits for them, and re-layouts  144 us
    all_gather x1, waiting for transfers between devices, local(): lax.all_gather(conv_weight_b, 'dp', axis=1, tiled=True)  127 us
    reduce_scatter x1, waiting for transfers between devices, local(): lax.psum_scatter(geglu_in_weight_grad.astype(jnp.bfloat16), 'dp', scatter...  123 us
    all_gather x8, waiting for transfers between devices, spread(): return lax.all_gather(array_in, 'mp', axis=1, tiled=True)  113 us
    all_gather x1, waiting for transfers between devices, local(): lax.all_gather(geglu_in_weight, 'dp', axis=0, tiled=True)  97.2 us
    all_gather x1, waiting for transfers between devices, local(): lax.all_gather(conv_weight_a, 'dp', axis=1, tiled=True)  96.6 us
  transfers between devices with their start and end apart: 51, of which 35 were waited for; matrix products, arithmetic and copies ran while one was open for 15% of the time, Pallas kernels for 0%

commit v1 on v0

v1 whole, which is shorter than its diff:
```python
import functools
import math

import jax
import jax.numpy as jnp
from jax import lax
from jax.experimental import pallas as pl
from jax.experimental.pallas import tpu as pltpu
from jax.sharding import Mesh
from jax.sharding import PartitionSpec as P

C = 1280
GROUPS = 32
HEAD = 64
TXT = 2048
TEMB = 1280
TXT_LEN = 77
TXT_PAD = 80
IMG_H = 16
IMG_W = 16
PIXELS = IMG_H * IMG_W
PROMPTS = 8


EPS = 1e-05
HIGH = lax.Precision.HIGHEST
NEG = -1e30
SCALE = 1.0 / math.sqrt(HEAD)
VMEM_LIMIT = 48 * 1024 * 1024


def narrow(array_in):
    return array_in.astype(jnp.bfloat16)


def wide(array_in):
    return array_in.astype(jnp.float32)


def product(operand_a, operand_b):
    return jnp.dot(operand_a, operand_b, preferred_element_type=jnp.float32)


def inner_rows(operand_a, operand_b):
    return lax.dot_general(
        operand_a, operand_b, (((0,), (0,)), ((), ())), preferred_element_type=jnp.float32
    )


def outer_cols(operand_a, operand_b):
    return lax.dot_general(
        operand_a, operand_b, (((1,), (1,)), ((), ())), preferred_element_type=jnp.float32
    )


def silu_back(grad_in, pre_act):
    sigmoid_value = jax.nn.sigmoid(pre_act)
    return grad_in * sigmoid_value * (1.0 + pre_act * (1.0 - sigmoid_value))


def geglu(value_part, gate_part):
    return value_part * jax.nn.gelu(gate_part, approximate=False)


def head_cols(head_index):
    return slice(head_index * HEAD, (head_index + 1) * HEAD)


def softmax_rows(scores):
    top_score = jnp.max(scores, axis=1, keepdims=True)
    weights = jnp.exp(scores - top_score)
    return weights / jnp.sum(weights, axis=1, keepdims=True)


def unit_back(query, keys, values, probs, grad_rows):
    grad_probs = outer_cols(grad_rows, values)
    delta = jnp.sum(probs * grad_probs, axis=1, keepdims=True)
    grad_scores = narrow(probs * (grad_probs - delta))
    grad_query = product(grad_scores, keys) * SCALE
    grad_keys = inner_rows(grad_scores, query) * SCALE
    grad_values = inner_rows(narrow(probs), grad_rows)
    return grad_query, grad_keys, grad_values


def self_units(row_count):
    units = [slice(s, s + PIXELS) for s in range(0, row_count - PIXELS + 1, PIXELS)]
    return units, slice(len(units) * PIXELS, row_count)


def self_kernel(qkv_ref, far_ref, out_ref):
    row_count, width = out_ref.shape
    whole, part = self_units(row_count)
    for rows in whole + [part]:
        outs = []
        for head_index in range(width // HEAD):
            cols = head_cols(head_index)
            query, keys, values = qkv_ref[0, rows, cols], qkv_ref[1, rows, cols], qkv_ref[2, rows, cols]
            if rows == part:
                keys = jnp.concatenate([keys, far_ref[0, :, cols]], axis=0)
                values = jnp.concatenate([values, far_ref[1, :, cols]], axis=0)
            probs = softmax_rows(outer_cols(query, keys) * SCALE)
            outs.append(product(narrow(probs), values))
        out_ref[rows, :] = narrow(jnp.concatenate(outs, axis=1))


def self_back_kernel(qkv_ref, far_ref, grad_ref, dqkv_ref, dfar_ref):
    row_count, width = grad_ref.shape
    whole, part = self_units(row_count)
    near = part.stop - part.start
    for rows in whole + [part]:
        parts = ([], [], [])
        for head_index in range(width // HEAD):
            cols = head_cols(head_index)
            query, keys, values = qkv_ref[0, rows, cols], qkv_ref[1, rows, cols], qkv_ref[2, rows, cols]
            if rows == part:
                keys = jnp.concatenate([keys, far_ref[0, :, cols]], axis=0)
                values = jnp.concatenate([values, far_ref[1, :, cols]], axis=0)
            probs = softmax_rows(outer_cols(query, keys) * SCALE)
            for kept, grad in zip(parts, unit_back(query, keys, values, probs, grad_ref[rows, cols])):
                kept.append(grad)
        grads = [jnp.concatenate(kept, axis=1) for kept in parts]
        dqkv_ref[0, rows, :] = narrow(grads[0])
        for index in (1, 2):
            if rows == part:
                dqkv_ref[index, rows, :] = narrow(grads[index][:near])
                dfar_ref[index - 1, :, :] = narrow(grads[index][near:])
            else:
                dqkv_ref[index, rows, :] = narrow(grads[index])


def cross_probs(query, keys, length):
    scores = outer_cols(query, keys) * SCALE
    live = lax.broadcasted_iota(jnp.int32, scores.shape, 1) < length
    return softmax_rows(jnp.where(live, scores, NEG))


def cross_kernel(prompt_ref, length_ref, query_ref, text_ref, out_ref):
    row_count, width = out_ref.shape
    whole, part = self_units(row_count)
    for slot, rows in enumerate(whole + [part]):
        prompt, length = prompt_ref[slot], length_ref[slot]
        keys, values = text_ref[0, prompt], text_ref[1, prompt]
        outs = []
        for head_index in range(width // HEAD):
            cols = head_cols(head_index)
            probs = cross_probs(query_ref[rows, cols], keys[:, cols], length)
            outs.append(product(narrow(probs), values[:, cols]))
        out_ref[rows, :] = narrow(jnp.concatenate(outs, axis=1))


def cross_back_kernel(prompt_ref, length_ref, query_ref, text_ref, grad_ref, dquery_ref, dtext_ref):
    row_count, width = grad_ref.shape
    whole, part = self_units(row_count)
    dtext_ref[...] = jnp.zeros_like(dtext_ref)
    for slot, rows in enumerate(whole + [part]):
        prompt, length = prompt_ref[slot], length_ref[slot]
        keys, values = text_ref[0, prompt], text_ref[1, prompt]
        parts = ([], [], [])
        for head_index in range(width // HEAD):
            cols = head_cols(head_index)
            query = query_ref[rows, cols]
            probs = cross_probs(query, keys[:, cols], length)
            for kept, grad in zip(
                parts, unit_back(query, keys[:, cols], values[:, cols], probs, grad_ref[rows, cols])
            ):
                kept.append(grad)
        grads = [jnp.concatenate(kept, axis=1) for kept in parts]
        dquery_ref[rows, :] = narrow(grads[0])
        dtext_ref[0, prompt] += grads[1]
        dtext_ref[1, prompt] += grads[2]


def in_vmem():
    return pl.BlockSpec(memory_space=pltpu.VMEM)


def in_smem():
    return pl.BlockSpec(memory_space=pltpu.SMEM)


def kernel_call(kernel, specs, outs, flops, *operands):
    shapes = [jax.ShapeDtypeStruct(shape, dtype) for shape, dtype in outs]
    moved = sum(o.size * o.dtype.itemsize for o in operands) + sum(
        math.prod(shape) * jnp.dtype(dtype).itemsize for shape, dtype in outs
    )
    results = pl.pallas_call(
        kernel,
        out_shape=shapes,
        in_specs=specs,
        out_specs=[in_vmem() for _ in shapes],
        compiler_params=pltpu.CompilerParams(vmem_limit_bytes=VMEM_LIMIT),
        cost_estimate=pl.CostEstimate(flops=flops, bytes_accessed=moved, transcendentals=flops // 128),
    )(*operands)
    return results[0] if len(results) == 1 else results


PAIR = ((0, 1), (1, 0))


def swap(array_in, axis):
    return lax.ppermute(array_in, axis, PAIR)


def pick(array_in, index, axis):
    return lax.dynamic_index_in_dim(array_in, index, axis, keepdims=False)


def owner_order(pieces):
    at_x, at_c = lax.axis_index("x") == 0, lax.axis_index("c") == 0
    half = [jnp.where(at_c, pieces[s], pieces[s ^ 1]) for s in range(4)]
    return [jnp.where(at_x, half[s], half[s ^ 2]) for s in range(4)]


def gather_mp(array_in):
    far = swap(array_in, "x")
    return owner_order([array_in, swap(array_in, "c"), far, swap(far, "c")])


def scatter_sum_mp(stacked):
    at_x, at_c = lax.axis_index("x"), lax.axis_index("c")
    kept = wide(pick(stacked, at_c, 1))
    got = wide(swap(pick(stacked, 1 - at_c, 1), "c"))
    total = kept + got
    return pick(total, at_x, 0) + wide(swap(narrow(pick(total, 1 - at_x, 0)), "x"))


def gather_eight(array_in):
    middle = array_in.shape[0] // 2
    by_h, by_x = swap(array_in, "h"), swap(array_in, "x")
    across = jnp.concatenate([swap(by_h[:middle], "x"), swap(by_x[middle:], "h")], axis=0)
    near = [array_in, by_x, by_h, across]
    far = [swap(piece, "c") for piece in near]
    at_c, at_h = lax.axis_index("c") == 0, lax.axis_index("h") == 0
    at_x = lax.axis_index("x") == 0
    half = [[jnp.where(at_c, n, f), jnp.where(at_c, f, n)] for n, f in zip(near, far)]
    quarter = [
        [jnp.where(at_x, half[s][c], half[s ^ 1][c]) for c in range(2)] for s in range(4)
    ]
    return [jnp.where(at_h, quarter[s][c], quarter[s ^ 2][c]) for s in range(4) for c in range(2)]


def scatter_sum_eight(stacked):
    at_h, at_x, at_c = lax.axis_index("h"), lax.axis_index("x"), lax.axis_index("c")
    total = wide(pick(stacked, at_c, 2)) + wide(swap(pick(stacked, 1 - at_c, 2), "c"))
    middle = total.shape[2] // 2
    upper, lower = total[:, :, :middle], total[:, :, middle:]
    upper = pick(upper, at_x, 1) + wide(swap(narrow(pick(upper, 1 - at_x, 1)), "x"))
    lower = pick(lower, at_h, 0) + wide(swap(narrow(pick(lower, 1 - at_h, 0)), "h"))
    upper = pick(upper, at_h, 0) + wide(swap(narrow(pick(upper, 1 - at_h, 0)), "h"))
    lower = pick(lower, at_x, 0) + wide(swap(narrow(pick(lower, 1 - at_x, 0)), "x"))
    return jnp.concatenate([upper, lower], axis=0)


def exchange_mp(stacked):
    place = 2 * lax.axis_index("x") + lax.axis_index("c")
    pieces = [pick(stacked, place ^ s, 0) for s in range(4)]
    far = swap(pieces[3], "c")
    return owner_order([pieces[0], swap(pieces[1], "c"), swap(pieces[2], "x"), swap(far, "x")])


def join_h(array_in, axis):
    other = swap(array_in, "h")
    first = lax.axis_index("h") == 0
    return jnp.concatenate(
        [jnp.where(first, array_in, other), jnp.where(first, other, array_in)], axis=axis
    )


def sum_g(array_in):
    size = lax.axis_size("g")
    total = array_in
    for step in range(1, size):
        total = total + rotate_g(array_in, step)
    return total


def gather_h(array_in, axis):
    other = swap(array_in, "h")
    first = lax.axis_index("h") == 0
    return jnp.stack(
        [jnp.where(first, array_in, other), jnp.where(first, other, array_in)], axis=axis
    )


def scatter_sum_h(array_in, axis):
    at_h = lax.axis_index("h")
    sent = narrow(pick(array_in, 1 - at_h, axis))
    return wide(pick(array_in, at_h, axis)) + wide(swap(sent, "h"))


def rotate_g(array_in, step):
    size = lax.axis_size("g")
    return lax.ppermute(array_in, "g", [(i, (i + step) % size) for i in range(size)])


def sum_pixels(array_in):
    size, at_g = lax.axis_size("g"), lax.axis_index("g")
    count, rows, width = array_in.shape
    share = scatter_sum_h(array_in.reshape(count, 2, rows // 2, width), 1)
    blocks = narrow(share).reshape(count, size, rows // 2 // size, width)
    total = pick(share.reshape(blocks.shape), at_g, 1)
    for step in range(1, size):
        total = total + wide(rotate_g(pick(blocks, (at_g + step) % size, 1), step))
    total = narrow(total)
    held = jnp.zeros_like(blocks)
    held = lax.dynamic_update_index_in_dim(held, total, at_g, 1)
    for step in range(1, size):
        got = rotate_g(total, step)
        held = lax.dynamic_update_index_in_dim(held, got, (at_g + size - step) % size, 1)
    return gather_h(held.reshape(count, rows // 2, width), 1).reshape(array_in.shape)


def shift_rows(array_in, to_next, count):
    size = lax.axis_size("g") * lax.axis_size("h")
    pairs = [(i, (i + 1) % size) for i in range(size)]
    if to_next:
        edge = lax.ppermute(array_in[-count:], ("g", "h"), pairs)
        return jnp.concatenate([edge, array_in[:-count]], axis=0)
    edge = lax.ppermute(array_in[:count], ("g", "h"), [(j, i) for i, j in pairs])
    return jnp.concatenate([array_in[count:], edge], axis=0)


def turn(array_in, count, forward):
    moved = jnp.roll(array_in, -count if forward else count, axis=0)
    return jnp.where(lax.axis_index("h") == 0, array_in, moved)


def conv_apply(act, weight):
    images = act.reshape(-1, IMG_H, IMG_W, act.shape[1])
    result = lax.conv_general_dilated(
        images,
        weight.reshape(3, 3, *weight.shape[1:]),
        (1, 1),
        ((1, 1), (1, 1)),
        dimension_numbers=("NHWC", "HWIO", "NHWC"),
        preferred_element_type=jnp.float32,
    )
    return result.reshape(act.shape[0], weight.shape[2])


def conv_back_input(grad, weight):
    images = grad.reshape(-1, IMG_H, IMG_W, grad.shape[1])
    result = lax.conv_general_dilated(
        images,
        weight.reshape(3, 3, *weight.shape[1:])[::-1, ::-1],
        (1, 1),
        ((1, 1), (1, 1)),
        dimension_numbers=("NHWC", "HWOI", "NHWC"),
        preferred_element_type=jnp.float32,
    )
    return result.reshape(grad.shape[0], weight.shape[1])


def conv_back_weight(act, grad):
    result = lax.conv_general_dilated(
        act.reshape(-1, IMG_H, IMG_W, act.shape[1]),
        grad.reshape(-1, IMG_H, IMG_W, grad.shape[1]),
        (1, 1),
        ((1, 1), (1, 1)),
        dimension_numbers=("CHWN", "IHWO", "HWNC"),
        preferred_element_type=jnp.float32,
    )
    return result.reshape(9, act.shape[1], grad.shape[1])


def local(
    latents,
    time_embed,
    text_states,
    item_prompt,
    prompt_length,
    out_grad,
    resnorm_gain_a,
    resnorm_bias_a,
    conv_weight_a,
    conv_bias_a,
    time_weight,
    time_bias,
    resnorm_gain_b,
    resnorm_bias_b,
    conv_weight_b,
    conv_bias_b,
    attn_norm_gain,
    attn_norm_bias,
    qkv_weight,
    attn_out_weight,
    attn_out_bias,
    cross_norm_gain,
    cross_norm_bias,
    cross_query_weight,
    cross_kv_weight,
    cross_out_weight,
    cross_out_bias,
    geglu_norm_gain,
    geglu_norm_bias,
    geglu_in_weight,
    geglu_in_bias,
    geglu_out_weight,
    geglu_out_bias,
):
    row_count, local_chans = latents.shape
    half_chans = local_chans // 2
    own_rows = row_count // 4
    pair_rows = 2 * row_count
    offset = PIXELS // 4
    near_rows = row_count % PIXELS
    pair_items = pair_rows // PIXELS
    g_count = lax.axis_size("g")
    g_index, h_index = lax.axis_index("g"), lax.axis_index("h")
    place = 2 * lax.axis_index("x") + lax.axis_index("c")
    dp_index = 2 * g_index + h_index
    item_total = time_embed.shape[0]
    first_item = g_index * pair_items
    group_width = C // GROUPS
    channel = jnp.arange(half_chans) // group_width
    same_group = (channel[:, None] == channel[None, :]).astype(jnp.float32)

    def half_of(vector):
        return lax.dynamic_slice_in_dim(vector, h_index * half_chans, half_chans, axis=0)

    def group_means(first_term, second_term):
        sums = jnp.stack([first_term, second_term]).reshape(2, pair_items, PIXELS, half_chans)
        sums = jnp.einsum("sic,cd->sid", sums.sum(axis=2), same_group, precision=HIGH)
        return sums[:, :, None, :] / (PIXELS * group_width)

    def by_item(array_in):
        return array_in.reshape(pair_items, PIXELS, half_chans)

    def group_forward(array_in):
        means = group_means(array_in, array_in * array_in)
        inverse = lax.rsqrt(means[1] - means[0] * means[0] + EPS)
        return ((by_item(array_in) - means[0]) * inverse).reshape(array_in.shape), inverse

    def group_backward(grad_in, normed, inverse, gain):
        scaled = grad_in * gain
        means = group_means(scaled, scaled * normed)
        result = inverse * (by_item(scaled) - means[0] - by_item(normed) * means[1])
        return result.reshape(grad_in.shape)

    def layer_forward(array_in):
        mean = jnp.mean(array_in, axis=1, keepdims=True)
        square = jnp.mean(array_in * array_in, axis=1, keepdims=True)
        inverse = lax.rsqrt(square - mean * mean + EPS)
        return ((array_in - mean) * inverse, inverse)

    def layer_backward(grad_in, normed, inverse, gain):
        scaled = grad_in * gain
        first = jnp.mean(scaled, axis=1, keepdims=True)
        second = jnp.mean(scaled * normed, axis=1, keepdims=True)
        return inverse * (scaled - first - normed * second)

    def full_chans(array_in):
        return jnp.concatenate(gather_mp(array_in), axis=1)

    def full_rows(array_in):
        return jnp.concatenate(gather_mp(array_in), axis=0)

    def collect_rows(array_in):
        return scatter_sum_mp(narrow(array_in).reshape(2, 2, own_rows, array_in.shape[1]))

    def collect_chans(array_in):
        rows, chans = array_in.shape
        split = narrow(array_in).reshape(rows, 4, chans // 4).transpose(1, 0, 2)
        return scatter_sum_mp(split.reshape(2, 2, rows, chans // 4))

    def pair_to_half(array_in):
        split = array_in.reshape(pair_rows, 2, half_chans)
        sent = narrow(pick(split, 1 - h_index, 1))
        return pick(split, h_index, 1) + wide(swap(sent, "h"))

    def half_to_rows(array_in, rows_type):
        split = array_in.reshape(2, row_count, half_chans)
        kept = pick(split, h_index, 0)
        got = swap(pick(split, 1 - h_index, 0).astype(rows_type), "h").astype(array_in.dtype)
        first = h_index == 0
        return jnp.concatenate([jnp.where(first, kept, got), jnp.where(first, got, kept)], axis=1)

    def rows_to_half(array_in):
        split = array_in.reshape(row_count, 2, half_chans)
        kept = pick(split, h_index, 1)
        got = swap(pick(split, 1 - h_index, 1), "h")
        first = h_index == 0
        return jnp.concatenate([jnp.where(first, kept, got), jnp.where(first, got, kept)], axis=0)

    conv_a_full = lax.all_gather(conv_weight_a, "g", axis=1, tiled=True)
    conv_b_full = lax.all_gather(conv_weight_b, "g", axis=1, tiled=True)
    square_held = jnp.concatenate(
        [
            qkv_weight,
            cross_query_weight[None],
            attn_out_weight.T[None],
            cross_out_weight.T[None],
        ],
        axis=0,
    )
    square_near = lax.all_gather(square_held, "g", axis=1, tiled=True)
    square_full = gather_h(square_near.reshape(6, g_count, -1, local_chans), 2)
    square_full = square_full.reshape(6, C, local_chans)
    qkv_full, cross_query_full = square_full[:3], square_full[3]
    attn_out_full, cross_out_full = square_full[4], square_full[5]

    def to_units(array_in):
        split = array_in.reshape(*array_in.shape[:2], 2, -1)
        kept = pick(split, h_index, 2)
        got = swap(pick(split, 1 - h_index, 2), "h")
        first = h_index == 0
        return jnp.concatenate(
            [jnp.where(first, kept, got), jnp.where(first, got, kept)], axis=0
        )

    def from_units(array_in):
        split = array_in.reshape(2, -1, *array_in.shape[1:])
        kept = pick(split, h_index, 0)
        got = swap(pick(split, 1 - h_index, 0), "h")
        first = h_index == 0
        return jnp.concatenate(
            [jnp.where(first, kept, got), jnp.where(first, got, kept)], axis=2
        )

    geglu_in_full = lax.all_gather(to_units(geglu_in_weight), "g", axis=0, tiled=True)
    geglu_out_full = lax.all_gather(
        to_units(geglu_out_weight.T[:, None, :])[:, 0], "g", axis=0, tiled=True
    )
    half_units = geglu_in_weight.shape[2] // 2
    unit_bias = lax.dynamic_slice_in_dim(geglu_in_bias, h_index * half_units, half_units, axis=1)
    vectors = full_chans(
        jnp.stack(
            [
                attn_norm_gain,
                attn_norm_bias,
                attn_out_bias,
                cross_norm_gain,
                cross_norm_bias,
                cross_out_bias,
                geglu_norm_gain,
                geglu_norm_bias,
            ]
        )
    )
    attn_gain, attn_bias, attn_shift, cross_gain, cross_bias, cross_shift, geglu_gain, geglu_bias = vectors

    latents_even = shift_rows(latents, True, offset)
    latents_turned = wide(turn(latents_even, near_rows, True))
    latent_in = wide(rows_to_half(latents_even))
    time_in = narrow(jax.nn.silu(wide(time_embed)))
    temb_local = time_weight.shape[0]
    time_slice = lax.dynamic_slice_in_dim(time_in, dp_index * temb_local, temb_local, axis=1)
    time_part = sum_g(product(time_slice, time_weight))
    time_part = lax.dynamic_slice_in_dim(time_part, first_item, pair_items, axis=0)
    gain_a, gain_b = half_of(resnorm_gain_a), half_of(resnorm_gain_b)
    normed_a, inverse_a = group_forward(latent_in)
    pre_a = normed_a * gain_a + half_of(resnorm_bias_a)
    act_a = full_chans(narrow(jax.nn.silu(pre_a)))
    middle_part = conv_apply(act_a, conv_a_full).reshape(pair_items, PIXELS, local_chans)
    middle_part = (middle_part + time_part[:, None, :]).reshape(pair_rows, local_chans)
    middle = pair_to_half(middle_part) + half_of(conv_bias_a + time_bias)
    normed_b, inverse_b = group_forward(middle)
    pre_b = normed_b * gain_b + half_of(resnorm_bias_b)
    act_b = full_chans(narrow(jax.nn.silu(pre_b)))
    resid_part = conv_apply(act_b, conv_b_full).reshape(2, row_count, local_chans)
    resid_sent = swap(narrow(pick(resid_part, 1 - h_index, 0)), "h")
    resid_part = pick(resid_part, h_index, 0) + wide(resid_sent)
    resid = latents_turned + turn(resid_part, near_rows, True) + conv_bias_b

    resid_full = full_chans(narrow(resid))
    normed_full, _ = layer_forward(wide(resid_full))
    full_one = narrow(normed_full * attn_gain + attn_bias)
    resid_one = wide(lax.dynamic_slice_in_dim(resid_full, place * own_rows, own_rows, axis=0))
    normed_one, inverse_one = layer_forward(resid_one)
    qkv_rows = narrow(
        jnp.einsum("rc,kcd->krd", full_one, qkv_full, preferred_element_type=jnp.float32)
    )
    far_rows = swap(qkv_rows[1:, row_count - near_rows :], "h")
    heads_flops = 4 * row_count * PIXELS * local_chans
    attended = kernel_call(
        self_kernel,
        [in_vmem(), in_vmem()],
        [((row_count, local_chans), jnp.bfloat16)],
        heads_flops,
        qkv_rows,
        far_rows,
    )
    resid_two = resid_one + collect_rows(outer_cols(attended, attn_out_full)) + attn_shift
    normed_two, inverse_two = layer_forward(resid_two)
    full_two = full_rows(narrow(normed_two * cross_gain + cross_bias))
    cross_query = narrow(product(full_two, cross_query_full))
    text_rows = jnp.pad(text_states, ((0, 0), (0, TXT_PAD - TXT_LEN), (0, 0)))
    text_rows = text_rows.reshape(PROMPTS * TXT_PAD, TXT)
    text_local = cross_kv_weight.shape[1]
    text_slice = lax.dynamic_slice_in_dim(text_rows, dp_index * text_local, text_local, axis=1)
    text_part = jnp.einsum(
        "pt,ktd->kpd", text_slice, cross_kv_weight, preferred_element_type=jnp.float32
    )
    text_kv = sum_pixels(text_part)
    text_kv = text_kv.reshape(2, PROMPTS, TXT_PAD, local_chans)
    slots = jnp.where(h_index == 0, 0, (row_count + PIXELS - 1) // PIXELS)
    slots = slots + jnp.arange(row_count // PIXELS + 1, dtype=jnp.int32)
    slots = jnp.where(jnp.arange(slots.shape[0]) == slots.shape[0] - 1, row_count // PIXELS, slots)
    slot_prompt = jnp.take(item_prompt, first_item + slots)
    slot_length = jnp.take(prompt_length, slot_prompt)
    cross_flops = 4 * row_count * TXT_PAD * local_chans
    cross_attended = kernel_call(
        cross_kernel,
        [in_smem(), in_smem(), in_vmem(), in_vmem()],
        [((row_count, local_chans), jnp.bfloat16)],
        cross_flops,
        slot_prompt,
        slot_length,
        cross_query,
        text_kv,
    )
    resid_three = resid_two + collect_rows(outer_cols(cross_attended, cross_out_full)) + cross_shift
    normed_three, inverse_three = layer_forward(resid_three)
    full_three = jnp.concatenate(
        gather_eight(narrow(normed_three * geglu_gain + geglu_bias)), axis=0
    )
    pre_ff = (
        jnp.einsum("rc,cjf->rjf", full_three, geglu_in_full, preferred_element_type=jnp.float32)
        + unit_bias
    )
    hidden = narrow(geglu(pre_ff[:, 0], pre_ff[:, 1]))
    row_place = jnp.arange(8)[:, None, None] == 4 * h_index + place
    block_part = product(hidden, geglu_out_full.T).reshape(8, own_rows, C)
    block_part = block_part + jnp.where(row_place, resid_three[None], 0.0)
    block_part = narrow(block_part).reshape(2, row_count, 4, local_chans).transpose(0, 2, 1, 3)
    block_part = block_part.reshape(2, 2, 2, row_count, local_chans)
    block_turned = narrow(scatter_sum_eight(block_part) + geglu_out_bias)
    block_out = shift_rows(turn(block_turned, near_rows, False), False, offset)

    geglu_out_bias_grad = jnp.sum(wide(out_grad), axis=0)
    grad_turned = turn(shift_rows(out_grad, True, offset), near_rows, True)
    grad_full = full_chans(join_h(grad_turned, 0))
    grad_three = wide(
        lax.dynamic_slice_in_dim(grad_full, (4 * h_index + place) * own_rows, own_rows, axis=0)
    )
    geglu_out_weight_part = narrow(inner_rows(grad_full, hidden))
    d_hidden = product(grad_full, geglu_out_full)
    _, geglu_pull = jax.vjp(geglu, pre_ff[:, 0], pre_ff[:, 1])
    d_value, d_gate = geglu_pull(d_hidden)
    d_pre = jnp.stack([d_value, d_gate], axis=1)
    geglu_in_bias_grad = jnp.sum(d_pre, axis=0)
    d_pre_low = narrow(d_pre)
    geglu_in_weight_part = narrow(
        jnp.einsum("rc,rjf->cjf", full_three, d_pre_low, preferred_element_type=jnp.float32)
    )
    d_norm_three = jnp.einsum(
        "rjf,cjf->rc", d_pre_low, geglu_in_full, preferred_element_type=jnp.float32
    )
    d_norm_three = scatter_sum_eight(narrow(d_norm_three).reshape(2, 2, 2, own_rows, C))
    geglu_norm_gain_grad = jnp.sum(d_norm_three * normed_three, axis=0)
    geglu_norm_bias_grad = jnp.sum(d_norm_three, axis=0)
    grad_two = grad_three + layer_backward(d_norm_three, normed_three, inverse_three, geglu_gain)
    cross_out_bias_grad = jnp.sum(grad_two, axis=0)
    cross_full = full_rows(narrow(grad_two))
    cross_out_weight_part = narrow(inner_rows(cross_full, cross_attended))
    d_cross = narrow(product(cross_full, cross_out_full))
    d_cross_query, text_grad_part = kernel_call(
        cross_back_kernel,
        [in_smem(), in_smem(), in_vmem(), in_vmem(), in_vmem()],
        [
            ((row_count, local_chans), jnp.bfloat16),
            ((2, PROMPTS, TXT_PAD, local_chans), jnp.float32),
        ],
        3 * cross_flops,
        slot_prompt,
        slot_length,
        cross_query,
        text_kv,
        d_cross,
    )
    cross_query_weight_part = narrow(inner_rows(full_two, d_cross_query))
    d_norm_two = collect_rows(outer_cols(d_cross_query, cross_query_full))
    cross_norm_gain_grad = jnp.sum(d_norm_two * normed_two, axis=0)
    cross_norm_bias_grad = jnp.sum(d_norm_two, axis=0)
    grad_one = grad_two + layer_backward(d_norm_two, normed_two, inverse_two, cross_gain)
    attn_out_bias_grad = jnp.sum(grad_one, axis=0)
    attn_full = full_rows(narrow(grad_one))
    attn_out_weight_part = narrow(inner_rows(attn_full, attended))
    d_attended = narrow(product(attn_full, attn_out_full))
    d_qkv, d_far = kernel_call(
        self_back_kernel,
        [in_vmem(), in_vmem(), in_vmem()],
        [
            ((3, row_count, local_chans), jnp.bfloat16),
            ((2, near_rows, local_chans), jnp.bfloat16),
        ],
        3 * heads_flops,
        qkv_rows,
        far_rows,
        d_attended,
    )
    d_near = wide(swap(d_far, "h")) + wide(d_qkv[1:, row_count - near_rows :])
    d_qkv = d_qkv.at[1:, row_count - near_rows :].set(narrow(d_near))
    qkv_weight_part = narrow(
        jnp.einsum("rc,krd->kcd", full_one, d_qkv, preferred_element_type=jnp.float32)
    )
    d_norm_one = collect_rows(
        jnp.einsum("krd,kcd->rc", d_qkv, qkv_full, preferred_element_type=jnp.float32)
    )
    attn_norm_gain_grad = jnp.sum(d_norm_one * normed_one, axis=0)
    attn_norm_bias_grad = jnp.sum(d_norm_one, axis=0)
    grad_zero = grad_one + layer_backward(d_norm_one, normed_one, inverse_one, attn_gain)

    zero_blocks = narrow(grad_zero).reshape(own_rows, 4, local_chans).transpose(1, 0, 2)
    zero_turned = jnp.concatenate(exchange_mp(zero_blocks), axis=0)
    zero_rows = turn(zero_turned, near_rows, False)
    conv_bias_b_grad = jnp.sum(wide(zero_rows), axis=0)
    zero_pair = join_h(zero_rows, 0)
    conv_weight_b_part = narrow(conv_back_weight(act_b, zero_pair))
    d_pre_b = silu_back(collect_chans(conv_back_input(zero_pair, conv_b_full)), pre_b)
    resnorm_gain_b_grad = jnp.sum(d_pre_b * normed_b, axis=0)
    resnorm_bias_b_grad = jnp.sum(d_pre_b, axis=0)
    d_middle = group_backward(d_pre_b, normed_b, inverse_b, gain_b)
    time_part_grad = by_item(d_middle).sum(axis=1)
    middle_pair = join_h(narrow(d_middle), 1)
    conv_weight_a_part = narrow(conv_back_weight(act_a, middle_pair))
    d_pre_a = silu_back(collect_chans(conv_back_input(middle_pair, conv_a_full)), pre_a)
    resnorm_gain_a_grad = jnp.sum(d_pre_a * normed_a, axis=0)
    resnorm_bias_a_grad = jnp.sum(d_pre_a, axis=0)
    d_latents = group_backward(d_pre_a, normed_a, inverse_a, gain_a)
    d_latents = wide(zero_rows) + half_to_rows(d_latents, jnp.bfloat16)
    latents_grad = shift_rows(d_latents, False, offset)

    row_vectors = jnp.stack(
        [
            attn_norm_gain_grad,
            attn_norm_bias_grad,
            attn_out_bias_grad,
            cross_norm_gain_grad,
            cross_norm_bias_grad,
            cross_out_bias_grad,
            geglu_norm_gain_grad,
            geglu_norm_bias_grad,
        ]
    )
    row_blocks = row_vectors.reshape(8, 4, local_chans).transpose(1, 0, 2)
    row_sums = scatter_sum_mp(narrow(row_blocks).reshape(2, 2, 8, local_chans))
    early = jnp.concatenate(
        [
            row_sums,
            geglu_out_bias_grad[None],
            conv_bias_b_grad[None],
        ],
        axis=0,
    )
    early = sum_g(early + swap(early, "h"))
    in_bias_grad = join_h(sum_g(geglu_in_bias_grad), 1)
    time_held = jnp.zeros((item_total, half_chans), jnp.float32)
    time_held = lax.dynamic_update_slice_in_dim(time_held, time_part_grad, first_item, axis=0)
    late = jnp.concatenate(
        [
            time_held,
            resnorm_gain_a_grad[None],
            resnorm_bias_a_grad[None],
            resnorm_gain_b_grad[None],
            resnorm_bias_b_grad[None],
        ],
        axis=0,
    )
    late = join_h(sum_g(late), 1)
    time_grad, norm_grads = late[:item_total], late[item_total:]
    time_bias_grad = jnp.sum(time_grad, axis=0)
    time_weight_grad = inner_rows(time_slice, narrow(time_grad))
    text_grad = sum_pixels(text_grad_part.reshape(2, PROMPTS * TXT_PAD, local_chans))
    cross_kv_weight_grad = jnp.stack(
        [inner_rows(text_slice, text_grad[0]), inner_rows(text_slice, text_grad[1])]
    )

    def to_owner(array_in, dim):
        return lax.psum_scatter(array_in, "g", scatter_dimension=dim, tiled=True)

    def pair_sum(parts):
        stacked = jnp.stack(parts).reshape(len(parts), g_count, 2, -1, local_chans)
        return narrow(scatter_sum_h(stacked, 2)).reshape(len(parts), -1, local_chans)

    geglu_out_weight_grad = from_units(to_owner(geglu_out_weight_part, 0)[:, None, :])
    geglu_out_weight_grad = wide(geglu_out_weight_grad)[:, 0].T
    geglu_in_weight_grad = wide(from_units(to_owner(geglu_in_weight_part, 0)))
    out_parts = pair_sum([cross_query_weight_part, cross_out_weight_part, attn_out_weight_part])
    out_grads = wide(to_owner(out_parts, 1))
    cross_query_weight_grad = out_grads[0]
    cross_out_weight_grad, attn_out_weight_grad = out_grads[1].T, out_grads[2].T
    qkv_weight_grad = wide(to_owner(pair_sum(list(qkv_weight_part)), 1))
    conv_weight_b_grad = wide(to_owner(conv_weight_b_part, 1))
    conv_weight_a_grad = wide(to_owner(conv_weight_a_part, 1))
    return (
        block_out,
        latents_grad,
        norm_grads[0],
        norm_grads[1],
        conv_weight_a_grad,
        time_bias_grad,
        time_weight_grad,
        time_bias_grad,
        norm_grads[2],
        norm_grads[3],
        conv_weight_b_grad,
        early[9],
        early[0],
        early[1],
        qkv_weight_grad,
        attn_out_weight_grad,
        early[2],
        early[3],
        early[4],
        cross_query_weight_grad,
        cross_kv_weight_grad,
        cross_out_weight_grad,
        early[5],
        early[6],
        early[7],
        geglu_in_weight_grad,
        in_bias_grad,
        geglu_out_weight_grad,
        early[8],
    )


DP, MP = ("g", "h"), ("x", "c")
EVERY = P()
ROWS = P(DP, MP)
VECTOR = P(MP)
STACK = P(None, DP, MP)
TURNED = P(MP, DP)
GATED = P(DP, None, MP)


def solution(mesh):
    dp_count, mp_count = mesh.shape["dp"], mesh.shape["mp"]
    split = Mesh(mesh.devices.reshape(dp_count // 2, 2, mp_count // 2, 2), ("g", "h", "x", "c"))
    return jax.shard_map(
        local,
        mesh=split,
        in_specs=(
            (ROWS, EVERY, EVERY, EVERY, EVERY, ROWS)
            + (VECTOR, VECTOR, STACK, VECTOR, ROWS, VECTOR, VECTOR, VECTOR, STACK, VECTOR)
            + (VECTOR, VECTOR, STACK, TURNED, VECTOR)
            + (VECTOR, VECTOR, ROWS, STACK, TURNED, VECTOR)
            + (VECTOR, VECTOR, GATED, P(None, MP), TURNED, VECTOR)
        ),
        out_specs=(
            (ROWS, ROWS, VECTOR, VECTOR, STACK, VECTOR, ROWS, VECTOR, VECTOR, VECTOR, STACK, VECTOR)
            + (VECTOR, VECTOR, STACK, TURNED, VECTOR)
            + (VECTOR, VECTOR, ROWS, STACK, TURNED, VECTOR)
            + (VECTOR, VECTOR, GATED, P(None, MP), TURNED, VECTOR)
        ),
        check_vma=False,
    )
```

time: 2080 us -> 1050 us (0.50)
  waiting for transfers between devices: 1310 us -> 350 us
  blocking collectives: 220 us -> 0 us
  local copies, waits for them, and re-layouts: 157 us -> 244 us
  matrix products: 234 us -> 170 us
  other arithmetic: 80.3 us -> 141 us
  starting transfers between devices: 52.5 us -> 98.5 us
  Pallas kernels: 0 us -> 22.3 us
    reduce_scatter x13 -> x6, waiting for transfers between devices: 458 us -> 0.03 us  [to_owner(): return lax.psum_scatter(array_in, 'g', scatter_dimension=dim, tiled=True)]
    all_gather x14 -> x5, waiting for transfers between devices: 510 us -> 127 us  [the longest x1 72.2 us: local(): conv_b_full = lax.all_gather(conv_weight_b, 'g', axis=1, tiled=True)]
    unnamed x34 -> x11, waiting for transfers between devices: 295 us -> 0.84 us
    ppermute x20 -> x111, waiting for transfers between devices: 47.7 us -> 222 us  [the longest x83 189 us: swap(): return lax.ppermute(array_in, axis, PAIR)]
    all_gather x4 -> x0, blocking collectives: 143 us -> none  [the longest x1 37.4 us: local(): lax.all_gather(cross_query_weight, 'dp', axis=0, tiled=True)]
    unnamed x414 -> x384, local copies, waits for them, and re-layouts: 144 us -> 43.8 us
    conv_general_dilated x0 -> x6, matrix products: none -> 90.2 us  [the longest x2 32.5 us: conv_apply(): lax.conv_general_dilated(images, weight.reshape(3, 3, *weight.shape[1:]),...]
    psum x7 -> x0, blocking collectives: 76.9 us -> none  [the longest x1 40.8 us: local(): lax.psum(vector_grads.astype(jnp.bfloat16), 'dp').astype(jnp.float32)]
  transfers between devices with their start and end apart: 51 -> 122, of which waited for: 35 -> 45; matrix products, arithmetic and copies ran while one was open for 15% -> 48% of each run, Pallas kernels for 0% -> 2%
where the time goes in v1:
time: 1050 us; the launch traced here: 1040 us
  waiting for transfers between devices  350 us (33%)
  local copies, waits for them, and re-layouts  244 us (23%)
  matrix products  170 us (16%)
  other arithmetic  141 us (13%)
  starting transfers between devices  98.5 us (9%)
  Pallas kernels  22.3 us (2%)
  between operations  17.7 us (2%)
    ppermute x83, waiting for transfers between devices, swap(): return lax.ppermute(array_in, axis, PAIR)  189 us
    all_gather x1, waiting for transfers between devices, local(): conv_b_full = lax.all_gather(conv_weight_b, 'g', axis=1, tiled=True)  72.2 us
    ppermute x83, starting transfers between devices, swap(): return lax.ppermute(array_in, axis, PAIR)  57 us
    convert_element_type x39, local copies, waits for them, and re-layouts, narrow(): return array_in.astype(jnp.bfloat16)  54.9 us
    unnamed x384, local copies, waits for them, and re-layouts  43.8 us
    all_gather x1, waiting for transfers between devices, local(): conv_a_full = lax.all_gather(conv_weight_a, 'g', axis=1, tiled=True)  42.5 us
    ppermute x24, starting transfers between devices, rotate_g(): lax.ppermute(array_in, 'g', [(i, (i + step) % size) for i in range(size)])  35.6 us
    conv_general_dilated x2, matrix products, conv_apply(): lax.conv_general_dilated(images, weight.reshape(3, 3, *weight.shape[1:]),...  32.5 us
  transfers between devices with their start and end apart: 122, of which 45 were waited for; matrix products, arithmetic and copies ran while one was open for 48% of the time, Pallas kernels for 2%

profile of v1, /device:TPU:0, one launch (start us, length us, event | category | flops | bytes accessed | tf_op | source)
XLA Modules:
  0.0 1042.7 jit_solution(514264533148599641)
XLA Ops:
  13.8 4.9 collective-permute-done
  19.7 8.2 collective-permute-done.1
  31.8 8.3 collective-permute-done.3
  57.6 42.5 %all-gather.7.cloned.1.call-done = bf16[9,640,320]{2,1,0:T(8,128)(2,1)} async-done(((bf16[9,160,320]{2,1,0:T(8,128)(2,1)}), bf16[9,640,320]{2,1,0:T(8,128)(2,1)}) %all-gather.7.cloned.1.call-update) | async-done | bytes 3686416 | tf_op jit(solution)/shard_map/all_gather | solution.py:485
  100.0 16.7 %fusion.54 = f32[5,16,16,320]{3,0,2,1:T(8,128)S(1)} fusion(bf16[3,3,640,320]{3,2,1,0:T(8,128)(2,1)} %bitcast.828, bf16[5,16,16,640]{3,2,1,0:T(8,128)(2,1)S(1)} %bitcast.800), kind=kOutput, calls=%fused_computation.106 | convolution fusion | flops 4333568000 | bytes 6963200 | tf_op jit(solution)/shard_map/conv_general_dilated | solution.py:330
  132.1 7.3 collective-permute-done.8
  174.5 72.2 %all-gather.9.cloned.1.call-done = bf16[9,640,320]{2,1,0:T(8,128)(2,1)} async-done(((bf16[9,160,320]{2,1,0:T(8,128)(2,1)}), bf16[9,640,320]{2,1,0:T(8,128)(2,1)}) %all-gather.9.cloned.1.call-update) | async-done | bytes 3686416 | tf_op jit(solution)/shard_map/all_gather | solution.py:486
  246.7 15.8 %fusion.50 = f32[5,16,16,320]{3,0,2,1:T(8,128)S(1)} fusion(bf16[3,3,640,320]{3,2,1,0:T(8,128)(2,1)} %bitcast.830, bf16[5,16,16,640]{3,2,1,0:T(8,128)(2,1)} %bitcast.802), kind=kOutput, calls=%fused_computation.102 | convolution fusion | flops 4333568000 | bytes 6963200 | tf_op jit(solution)/shard_map/conv_general_dilated | solution.py:330
  282.7 9.1 collective-permute-done.26
  305.1 5.6 convolution_convert_fusion.9
  356.3 5.3 collective-permute-done.22
  402.7 9.6 collective-permute-done.55
  412.4 8.2 collective-permute-done.35
  439.0 5.3 broadcast_select_fusion.4
  444.3 6.8 concatenate.159
  454.6 4.9 collective-permute-done.42
  459.7 6.9 fusion.80
  479.2 12.7 %all-gather.13.cloned.1.call-done = bf16[1280,2,640]{2,0,1:T(8,128)(2,1)} async-done(((bf16[320,2,640]{2,0,1:T(8,128)(2,1)}), bf16[1280,2,640]{2,0,1:T(8,128)(2,1)}) %all-gather.13.cloned.1.call-update) | async-done | bytes 3276816 | tf_op jit(solution)/shard_map/all_gather | solution.py:520
  491.8 7.5 convolution_add_fusion
  499.4 8.3 multiply_bitcast_fusion
  509.4 4.2 convolution_convert_fusion.2
  513.6 6.4 fusion.22
  525.7 6.8 negate_multiply_fusion
  532.7 8.5 fusion
  544.9 10.5 %add_convert_fusion = bf16[8,160,1280]{2,1,0:T(8,128)(2,1)} fusion(f32[160,1280]{1,0:T(8,128)S(1)} %get-tuple-element.364, pred[8]{0:T(512)(128)(4,1)S(1)} %iota_compare_fusion.1, bf16[1280,1,640]{2,0,1:T(8,128)(2,1)S(1)} %copy-done.175, f32[8,160,640]{2,1,0:T(8,128)S(1)} %bitcast.789, f32[8,160,640]{2,1,0:T(8,128)S(1)} %bitcast.788, ...), kind=kOutput, calls=%fused_computation.11 | convolution fusion | flops 2153676800 | bytes 15564808 | tf_op jit(solution)/shard_map/dot_general | solution.py:41
  555.4 8.3 convolution_convert_fusion
  563.7 8.8 reshape.708
  572.5 7.6 copy.769
  609.7 6.8 collective-permute-done.47
  626.9 9.7 collective-permute-done.63
  646.1 7.7 shard_map.538
  712.1 8.2 shard_map.539
  746.4 25.9 %collective-permute-done.96 = bf16[3,4,160,320]{3,2,1,0:T(8,128)(2,1)S(1)} collective-permute-done((bf16[3,4,160,320]{3,2,1,0:T(8,128)(2,1)S(1)}, bf16[3,4,160,320]{3,2,1,0:T(8,128)(2,1)S(1)}, u32[]{:S(2)}, u32[]{:S(2)}) %collective-permute-start.96) | collective-permute-done | bytes 1228832 | tf_op jit(solution)/shard_map/ppermute | solution.py:201
  777.7 5.2 copy.819
  792.7 25.7 %collective-permute-done.95 = bf16[3,4,160,320]{3,2,1,0:T(8,128)(2,1)} collective-permute-done((bf16[3,4,160,320]{3,2,1,0:T(8,128)(2,1)S(1)}, bf16[3,4,160,320]{3,2,1,0:T(8,128)(2,1)}, u32[]{:S(2)}, u32[]{:S(2)}) %collective-permute-start.95) | collective-permute-done | bytes 1228832 | tf_op jit(solution)/shard_map/ppermute | solution.py:201
  827.1 6.3 collective-permute-done.77
  833.6 15.8 %fusion.59 = bf16[3,3,640,320]{2,3,1,0:T(8,128)(2,1)} fusion(bf16[5,16,16,640]{3,2,1,0:T(8,128)(2,1)S(1)} %bitcast.803, bf16[5,16,16,320]{3,2,1,0:T(8,128)(2,1)S(1)} %bitcast.778), kind=kOutput, calls=%fused_computation.116 | convolution fusion | flops 4335411200 | bytes 6144000 | tf_op jit(solution)/shard_map/conv_general_dilated | solution.py:355
  849.4 7.8 copy.816
  858.4 12.9 %select_convert_fusion.1 = bf16[16,40,3,640]{3,1,2,0:T(8,128)(2,1)S(1)} fusion(pred[40,3]{0,1:T(4,128)(4,1)S(1)} %copy-done.178, bf16[3,3,640,320]{3,2,1,0:T(8,128)(2,1)} %bitcast.831, bf16[16,5,8,5,320]{4,0,3,2,1:T(8,128)(2,1)S(1)} %fusion.62), kind=kOutput, calls=%fused_computation.19 | convolution fusion | flops 6785433600 | bytes 8192120 | tf_op jit(solution)/shard_map/conv_general_dilated | solution.py:343
  888.4 9.3 collective-permute-done.79
  906.4 7.1 collective-permute-done.80
  917.3 16.0 %fusion.56 = bf16[3,3,640,320]{2,3,1,0:T(8,128)(2,1)} fusion(bf16[5,16,16,640]{3,2,1,0:T(8,128)(2,1)S(1)} %bitcast.801, bf16[5,16,16,320]{3,2,1,0:T(8,128)(2,1)S(1)} %bitcast.776), kind=kOutput, calls=%fused_computation.115 | convolution fusion | flops 4335411200 | bytes 6144000 | tf_op jit(solution)/shard_map/conv_general_dilated | solution.py:355
  933.3 7.8 copy.813
  950.3 13.0 %select_convert_fusion = bf16[16,40,3,640]{3,1,2,0:T(8,128)(2,1)S(1)} fusion(pred[40,3]{0,1:T(4,128)(4,1)S(1)} %copy-done.178, bf16[3,3,640,320]{3,2,1,0:T(8,128)(2,1)} %bitcast.829, bf16[16,5,8,5,320]{4,0,3,2,1:T(8,128)(2,1)S(1)} %fusion.63), kind=kOutput, calls=%fused_computation.18 | convolution fusion | flops 6785433600 | bytes 8192120 | tf_op jit(solution)/shard_map/conv_general_dilated | solution.py:343
  965.3 4.7 convert_element_type.642
  970.0 5.0 copy.808
  991.1 6.3 collective-permute-done.82
  1018.7 4.6 collective-permute-done.83
  (974 shorter events, 492.0 us)
Async XLA Ops:
  7.2 92.8 %all-gather.7.cloned.1.call-start = ((), (), s32[]{:S(2)}) async-start(), calls=%async_computation.6 | async-start | bytes 5529600 | tf_op jit(solution)/shard_map/all_gather | solution.py:485
  8.0 156.9 %all-gather.11.cloned.1.call-start = ((), (), s32[]{:S(2)}) async-start(), calls=%async_computation.8 | async-start | bytes 3686400 | tf_op jit(solution)/shard_map/all_gather | solution.py:496
  10.3 236.5 %all-gather.9.cloned.1.call-start = ((), (), s32[]{:S(2)}) async-start(), calls=%async_computation.7 | async-start | bytes 5529600 | tf_op jit(solution)/shard_map/all_gather | solution.py:486
  31.8 21.8 %collective-permute-start.2 = (bf16[1280,160]{0,1:T(8,128)(2,1)}, bf16[1280,160]{0,1:T(8,128)(2,1)}, u32[]{:S(2)}, u32[]{:S(2)}) collective-permute-start(bf16[1280,160]{0,1:T(8,128)(2,1)} %copy.726), channel_id=1, source_target_pairs={{0,1},{1,0},{2,3},{3,2},{4,5},{5,4},{6,7},{7,6},{8,9},{9,8},{10,11... | collective-permute-start | bytes 1228808 | tf_op jit(solution)/shard_map/ppermute | solution.py:201
  44.3 415.4 %all-gather.15.cloned.1.call-start = ((), (), s32[]{:S(2)}) async-start(), calls=%async_computation.16 | async-start | bytes 2048000 | tf_op jit(solution)/shard_map/all_gather | solution.py:521
  147.0 15.6 %collective-permute-start.18 = (f32[8,320]{1,0:T(8,128)S(1)}, f32[8,320]{1,0:T(8,128)S(1)}, u32[]{:S(2)}, u32[]{:S(2)}) collective-permute-start(f32[8,320]{1,0:T(8,128)S(1)} %stack.158), channel_id=1, source_target_pairs={{0,2},{2,0},{1,3},{3,1},{4,6},{6,4},{5,7},{7,5},{8,10},{10,8},{9,1... | collective-permute-start | bytes 30728 | tf_op jit(solution)/shard_map/ppermute | solution.py:201
  147.6 131.2 %collective-permute-start.17 = (f32[8,320]{1,0:T(8,128)S(1)}, f32[8,320]{1,0:T(8,128)S(1)}, u32[]{:S(2)}, u32[]{:S(2)}) collective-permute-start(f32[8,320]{1,0:T(8,128)S(1)} %stack.158), channel_id=1, source_target_pairs={{0,1},{1,0},{2,3},{3,2},{4,5},{5,4},{6,7},{7,6},{8,9},{9,8},{10,11... | collective-permute-start | bytes 30728 | tf_op jit(solution)/shard_map/ppermute | solution.py:201
  149.3 220.6 %collective-permute-start.52 = (bf16[64,320]{1,0:T(8,128)(2,1)}, bf16[64,320]{1,0:T(8,128)(2,1)S(1)}, u32[]{:S(2)}, u32[]{:S(2)}) collective-permute-start(bf16[64,320]{1,0:T(8,128)(2,1)} %copy.852), channel_id=1, source_target_pairs={{0,4},{4,8},{8,12},{12,16},{16,20},{20,24},{24,28},{28,0},{1,5},{5... | collective-permute-start | bytes 122888 | tf_op jit(solution)/shard_map/ppermute | solution.py:317
  162.6 116.7 %collective-permute-start.19 = (f32[8,320]{1,0:T(8,128)S(1)}, f32[8,320]{1,0:T(8,128)S(1)}, u32[]{:S(2)}, u32[]{:S(2)}) collective-permute-start(f32[8,320]{1,0:T(8,128)S(1)} %collective-permute-done.18), channel_id=1, source_target_pairs={{0,1},{1,0},{2,3},{3,2},{4,5},{5,4},{6,7},{7,6},{8,9},{9,8},{10,11... | collective-permute-start | bytes 30728 | tf_op jit(solution)/shard_map/ppermute | solution.py:201
  164.9 129.7 %collective-permute-start.16 = (bf16[6,4,160,320]{3,2,1,0:T(8,128)(2,1)}, bf16[6,4,160,320]{3,2,1,0:T(8,128)(2,1)}, u32[]{:S(2)}, u32[]{:S(2)}) collective-permute-start(bf16[6,4,160,320]{3,2,1,0:T(8,128)(2,1)} %bitcast.792), channel_id=1, source_target_pairs={{0,4},{4,0},{1,5},{5,1},{2,6},{6,2},{3,7},{7,3},{8,12},{12,8},{9,1... | collective-permute-start | bytes 7372808 | tf_op jit(solution)/shard_map/ppermute | solution.py:201
  326.2 24.4 %collective-permute-start.21 = (bf16[2,160,1280]{2,1,0:T(8,128)(2,1)}, bf16[2,160,1280]{2,1,0:T(8,128)(2,1)}, u32[]{:S(2)}, u32[]{:S(2)}) collective-permute-start(bf16[2,160,1280]{2,1,0:T(8,128)(2,1)} %dynamic-slice_bitcast_fusion.9), channel_id=1, source_target_pairs={{0,1},{1,0},{2,3},{3,2},{4,5},{5,4},{6,7},{7,6},{8,9},{9,8},{10,11... | collective-permute-start | bytes 2457608 | tf_op jit(solution)/shard_map/ppermute | solution.py:201
  334.4 49.2 %collective-permute-start.45 = (bf16[160,1,640]{2,0,1:T(8,128)(2,1)}, bf16[160,1,640]{2,0,1:T(8,128)(2,1)}, u32[]{:S(2)}, u32[]{:S(2)}) collective-permute-start(bf16[160,1,640]{2,0,1:T(8,128)(2,1)} %bitcast.707), channel_id=1, source_target_pairs={{0,4},{4,0},{1,5},{5,1},{2,6},{6,2},{3,7},{7,3},{8,12},{12,8},{9,1... | collective-permute-start | bytes 614408 | tf_op jit(solution)/shard_map/ppermute | solution.py:201
  355.4 18.1 %collective-permute-start.33 = (bf16[2,320,320]{2,1,0:T(8,128)(2,1)}, bf16[2,320,320]{2,1,0:T(8,128)(2,1)}, u32[]{:S(2)}, u32[]{:S(2)}) collective-permute-start(bf16[2,320,320]{2,1,0:T(8,128)(2,1)} %bitcast.63), channel_id=1, source_target_pairs={{0,4},{4,0},{1,5},{5,1},{2,6},{6,2},{3,7},{7,3},{8,12},{12,8},{9,1... | collective-permute-start | bytes 1228808 | tf_op jit(solution)/shard_map/ppermute | solution.py:201
  385.4 106.4 %all-gather.13.cloned.1.call-start = ((), (), s32[]{:S(2)}) async-start(), calls=%async_computation.9 | async-start | bytes 4096000 | tf_op jit(solution)/shard_map/all_gather | solution.py:520
  391.0 21.4 %collective-permute-start.55 = (bf16[1280,320]{0,1:T(8,128)(2,1)}, bf16[1280,320]{0,1:T(8,128)(2,1)}, u32[]{:S(2)}, u32[]{:S(2)}) collective-permute-start(bf16[1280,320]{0,1:T(8,128)(2,1)} %copy.775), channel_id=1, source_target_pairs={{0,2},{2,0},{1,3},{3,1},{4,6},{6,4},{5,7},{7,5},{8,10},{10,8},{9,1... | collective-permute-start | bytes 2457608 | tf_op jit(solution)/shard_map/ppermute | solution.py:201
  395.9 24.6 %collective-permute-start.35 = (bf16[160,1280]{1,0:T(8,128)(2,1)}, bf16[160,1280]{1,0:T(8,128)(2,1)}, u32[]{:S(2)}, u32[]{:S(2)}) collective-permute-start(bf16[160,1280]{1,0:T(8,128)(2,1)} %fusion.125), channel_id=1, source_target_pairs={{0,2},{2,0},{1,3},{3,1},{4,6},{6,4},{5,7},{7,5},{8,10},{10,8},{9,1... | collective-permute-start | bytes 1228808 | tf_op jit(solution)/shard_map/ppermute | solution.py:201
  400.0 26.2 %collective-permute-start.44 = (bf16[160,2,640]{2,0,1:T(8,128)(2,1)}, bf16[160,2,640]{2,0,1:T(8,128)(2,1)}, u32[]{:S(2)}, u32[]{:S(2)}) collective-permute-start(bf16[160,2,640]{2,0,1:T(8,128)(2,1)} %bitcast.706), channel_id=1, source_target_pairs={{0,4},{4,0},{1,5},{5,1},{2,6},{6,2},{3,7},{7,3},{8,12},{12,8},{9,1... | collective-permute-start | bytes 1228808 | tf_op jit(solution)/shard_map/ppermute | solution.py:201
  402.6 28.2 %collective-permute-start.54 = (bf16[1280,320]{0,1:T(8,128)(2,1)}, bf16[1280,320]{0,1:T(8,128)(2,1)}, u32[]{:S(2)}, u32[]{:S(2)}) collective-permute-start(bf16[1280,320]{0,1:T(8,128)(2,1)} %copy.775), channel_id=1, source_target_pairs={{0,1},{1,0},{2,3},{3,2},{4,5},{5,4},{6,7},{7,6},{8,9},{9,8},{10,11... | collective-permute-start | bytes 2457608 | tf_op jit(solution)/shard_map/ppermute | solution.py:201
  412.4 20.7 %collective-permute-start.56 = (bf16[1280,320]{0,1:T(8,128)(2,1)}, bf16[1280,320]{0,1:T(8,128)(2,1)}, u32[]{:S(2)}, u32[]{:S(2)}) collective-permute-start(bf16[1280,320]{0,1:T(8,128)(2,1)} %collective-permute-done.55), channel_id=1, source_target_pairs={{0,1},{1,0},{2,3},{3,2},{4,5},{5,4},{6,7},{7,6},{8,9},{9,8},{10,11... | collective-permute-start | bytes 2457608 | tf_op jit(solution)/shard_map/ppermute | solution.py:201
  428.3 250.5 %reduce-scatter.17.cloned.1.call-start = ((), (), s32[]{:S(2)}) async-start(), calls=%async_computation.15 | async-start | bytes 2048000 | tf_op jit(solution)/shard_map/reduce_scatter | solution.py:770
  435.3 15.8 %collective-permute-start.37 = (bf16[160,1280]{1,0:T(8,128)(2,1)}, bf16[160,1280]{1,0:T(8,128)(2,1)}, u32[]{:S(2)}, u32[]{:S(2)}) collective-permute-start(bf16[160,1280]{1,0:T(8,128)(2,1)} %add_convert_fusion.1), channel_id=1, source_target_pairs={{0,2},{2,0},{1,3},{3,1},{4,6},{6,4},{5,7},{7,5},{8,10},{10,8},{9,1... | collective-permute-start | bytes 1228808 | tf_op jit(solution)/shard_map/ppermute | solution.py:201
  451.0 16.2 %collective-permute-start.36 = (bf16[160,1280]{1,0:T(8,128)(2,1)}, bf16[160,1280]{1,0:T(8,128)(2,1)S(1)}, u32[]{:S(2)}, u32[]{:S(2)}) collective-permute-start(bf16[160,1280]{1,0:T(8,128)(2,1)} %add_convert_fusion.1), channel_id=1, source_target_pairs={{0,1},{1,0},{2,3},{3,2},{4,5},{5,4},{6,7},{7,6},{8,9},{9,8},{10,11... | collective-permute-start | bytes 1228808 | tf_op jit(solution)/shard_map/ppermute | solution.py:201
  521.7 58.3 %collective-permute-start.106 = (f32[2,640]{1,0:T(2,128)S(1)}, f32[2,640]{1,0:T(2,128)S(1)}, u32[]{:S(2)}, u32[]{:S(2)}) collective-permute-start(f32[2,640]{1,0:T(2,128)S(1)} %fusion.1), channel_id=1, source_target_pairs={{0,8},{8,16},{16,24},{24,0},{1,9},{9,17},{17,25},{25,1},{2,10},{10... | collective-permute-start | bytes 15368 | tf_op jit(solution)/shard_map/ppermute | solution.py:293
  521.7 58.3 %collective-permute-start.107 = (f32[2,640]{1,0:T(2,128)S(1)}, f32[2,640]{1,0:T(2,128)S(1)}, u32[]{:S(2)}, u32[]{:S(2)}) collective-permute-start(f32[2,640]{1,0:T(2,128)S(1)} %fusion.1), channel_id=1, source_target_pairs={{0,16},{8,24},{16,0},{24,8},{1,17},{9,25},{17,1},{25,9},{2,18},{10... | collective-permute-start | bytes 15368 | tf_op jit(solution)/shard_map/ppermute | solution.py:293
  523.0 57.0 %collective-permute-start.108 = (f32[2,640]{1,0:T(2,128)S(1)}, f32[2,640]{1,0:T(2,128)S(1)}, u32[]{:S(2)}, u32[]{:S(2)}) collective-permute-start(f32[2,640]{1,0:T(2,128)S(1)} %fusion.1), channel_id=1, source_target_pairs={{0,24},{8,0},{16,8},{24,16},{1,25},{9,1},{17,9},{25,17},{2,26},{10... | collective-permute-start | bytes 15368 | tf_op jit(solution)/shard_map/ppermute | solution.py:293
  532.6 413.5 %reduce-scatter.15.cloned.1.call-start = ((), (), s32[]{:S(2)}) async-start(), calls=%async_computation.14 | async-start | bytes 4096000 | tf_op jit(solution)/shard_map/reduce_scatter | solution.py:770
  542.4 47.5 %collective-permute-start.57 = (bf16[2,2,160,1280]{3,2,1,0:T(8,128)(2,1)}, bf16[2,2,160,1280]{3,2,1,0:T(8,128)(2,1)}, u32[]{:S(2)}, u32[]{:S(2)}) collective-permute-start(bf16[2,2,160,1280]{3,2,1,0:T(8,128)(2,1)} %dynamic-slice_bitcast_fusion), channel_id=1, source_target_pairs={{0,1},{1,0},{2,3},{3,2},{4,5},{5,4},{6,7},{7,6},{8,9},{9,8},{10,11... | collective-permute-start | bytes 4915208 | tf_op jit(solution)/shard_map/ppermute | solution.py:201
  589.2 392.8 %reduce-scatter.13.cloned.1.call-start = ((), (), s32[]{:S(2)}) async-start(), calls=%async_computation.13 | async-start | bytes 1843200 | tf_op jit(solution)/shard_map/reduce_scatter | solution.py:770
  603.5 21.9 %collective-permute-start.49 = (bf16[2,320,320]{2,1,0:T(8,128)(2,1)S(1)}, bf16[2,320,320]{2,1,0:T(8,128)(2,1)S(1)}, u32[]{:S(2)}, u32[]{:S(2)}) collective-permute-start(bf16[2,320,320]{2,1,0:T(8,128)(2,1)S(1)} %fusion.116), channel_id=1, source_target_pairs={{0,4},{4,0},{1,5},{5,1},{2,6},{6,2},{3,7},{7,3},{8,12},{12,8},{9,1... | collective-permute-start | bytes 1228808 | tf_op jit(solution)/shard_map/ppermute | solution.py:201
  606.2 15.9 %collective-permute-start.59 = (bf16[80,1280]{1,0:T(8,128)(2,1)S(1)}, bf16[80,1280]{1,0:T(8,128)(2,1)S(1)}, u32[]{:S(2)}, u32[]{:S(2)}) collective-permute-start(bf16[80,1280]{1,0:T(8,128)(2,1)S(1)} %fusion.145), channel_id=1, source_target_pairs={{0,4},{4,0},{1,5},{5,1},{2,6},{6,2},{3,7},{7,3},{8,12},{12,8},{9,1... | collective-permute-start | bytes 614408 | tf_op jit(solution)/shard_map/ppermute | solution.py:201
  663.4 24.6 %collective-permute-start.97 = (bf16[2,320,320]{2,1,0:T(8,128)(2,1)}, bf16[2,320,320]{2,1,0:T(8,128)(2,1)}, u32[]{:S(2)}, u32[]{:S(2)}) collective-permute-start(bf16[2,320,320]{2,1,0:T(8,128)(2,1)} %fusion.117), channel_id=1, source_target_pairs={{0,4},{4,0},{1,5},{5,1},{2,6},{6,2},{3,7},{7,3},{8,12},{12,8},{9,1... | collective-permute-start | bytes 1228808 | tf_op jit(solution)/shard_map/ppermute | solution.py:201
  693.0 15.4 %collective-permute-start.67 = (bf16[160,1280]{1,0:T(8,128)(2,1)S(1)}, bf16[160,1280]{1,0:T(8,128)(2,1)S(1)}, u32[]{:S(2)}, u32[]{:S(2)}) collective-permute-start(bf16[160,1280]{1,0:T(8,128)(2,1)S(1)} %convert_element_type.618), channel_id=1, source_target_pairs={{0,1},{1,0},{2,3},{3,2},{4,5},{5,4},{6,7},{7,6},{8,9},{9,8},{10,11... | collective-permute-start | bytes 1228808 | tf_op jit(solution)/shard_map/ppermute | solution.py:201
  704.6 16.0 %collective-permute-start.101 = (bf16[2,80,320]{2,1,0:T(8,128)(2,1)}, bf16[2,80,320]{2,1,0:T(8,128)(2,1)}, u32[]{:S(2)}, u32[]{:S(2)}) collective-permute-start(bf16[2,80,320]{2,1,0:T(8,128)(2,1)} %get-tuple-element.327), channel_id=1, source_target_pairs={{0,8},{8,16},{16,24},{24,0},{1,9},{9,17},{17,25},{25,1},{2,10},{10... | collective-permute-start | bytes 307208 | tf_op jit(solution)/shard_map/ppermute | solution.py:293
  704.6 32.9 %collective-permute-start.102 = (bf16[2,80,320]{2,1,0:T(8,128)(2,1)}, bf16[2,80,320]{2,1,0:T(8,128)(2,1)}, u32[]{:S(2)}, u32[]{:S(2)}) collective-permute-start(bf16[2,80,320]{2,1,0:T(8,128)(2,1)} %get-tuple-element.327), channel_id=1, source_target_pairs={{0,16},{8,24},{16,0},{24,8},{1,17},{9,25},{17,1},{25,9},{2,18},{10... | collective-permute-start | bytes 307208 | tf_op jit(solution)/shard_map/ppermute | solution.py:293
  706.8 32.2 %collective-permute-start.103 = (bf16[2,80,320]{2,1,0:T(8,128)(2,1)}, bf16[2,80,320]{2,1,0:T(8,128)(2,1)}, u32[]{:S(2)}, u32[]{:S(2)}) collective-permute-start(bf16[2,80,320]{2,1,0:T(8,128)(2,1)} %get-tuple-element.327), channel_id=1, source_target_pairs={{0,24},{8,0},{16,8},{24,16},{1,25},{9,1},{17,9},{25,17},{2,26},{10... | collective-permute-start | bytes 307208 | tf_op jit(solution)/shard_map/ppermute | solution.py:293
  737.1 35.1 %collective-permute-start.96 = (bf16[3,4,160,320]{3,2,1,0:T(8,128)(2,1)S(1)}, bf16[3,4,160,320]{3,2,1,0:T(8,128)(2,1)S(1)}, u32[]{:S(2)}, u32[]{:S(2)}) collective-permute-start(bf16[3,4,160,320]{3,2,1,0:T(8,128)(2,1)S(1)} %dynamic-slice_bitcast_fusion.2), channel_id=1, source_target_pairs={{0,4},{4,0},{1,5},{5,1},{2,6},{6,2},{3,7},{7,3},{8,12},{12,8},{9,1... | collective-permute-start | bytes 3686408 | tf_op jit(solution)/shard_map/ppermute | solution.py:201
  740.6 48.1 %collective-permute-start.104 = (bf16[2,320,320]{2,1,0:T(8,128)(2,1)}, bf16[2,320,320]{2,1,0:T(8,128)(2,1)}, u32[]{:S(2)}, u32[]{:S(2)}) collective-permute-start(bf16[2,320,320]{2,1,0:T(8,128)(2,1)} %bitcast.215), channel_id=1, source_target_pairs={{0,4},{4,0},{1,5},{5,1},{2,6},{6,2},{3,7},{7,3},{8,12},{12,8},{9,1... | collective-permute-start | bytes 1228808 | tf_op jit(solution)/shard_map/ppermute | solution.py:201
  745.7 39.3 %collective-permute-start.72 = (bf16[160,1280]{1,0:T(8,128)(2,1)}, bf16[160,1280]{1,0:T(8,128)(2,1)}, u32[]{:S(2)}, u32[]{:S(2)}) collective-permute-start(bf16[160,1280]{1,0:T(8,128)(2,1)} %fusion.129), channel_id=1, source_target_pairs={{0,2},{2,0},{1,3},{3,1},{4,6},{6,4},{5,7},{7,5},{8,10},{10,8},{9,1... | collective-permute-start | bytes 1228808 | tf_op jit(solution)/shard_map/ppermute | solution.py:201
  773.8 212.8 %reduce-scatter.11.cloned.1.call-start = ((), (), s32[]{:S(2)}) async-start(), calls=%async_computation.12 | async-start | bytes 1843200 | tf_op jit(solution)/shard_map/reduce_scatter | solution.py:770
  784.7 33.7 %collective-permute-start.95 = (bf16[3,4,160,320]{3,2,1,0:T(8,128)(2,1)S(1)}, bf16[3,4,160,320]{3,2,1,0:T(8,128)(2,1)}, u32[]{:S(2)}, u32[]{:S(2)}) collective-permute-start(bf16[3,4,160,320]{3,2,1,0:T(8,128)(2,1)S(1)} %dynamic-slice_bitcast_fusion.3), channel_id=1, source_target_pairs={{0,4},{4,0},{1,5},{5,1},{2,6},{6,2},{3,7},{7,3},{8,12},{12,8},{9,1... | collective-permute-start | bytes 3686408 | tf_op jit(solution)/shard_map/ppermute | solution.py:201
  790.0 31.3 %collective-permute-start.73 = (bf16[160,320]{1,0:T(8,128)(2,1)S(1)}, bf16[160,320]{1,0:T(8,128)(2,1)S(1)}, u32[]{:S(2)}, u32[]{:S(2)}) collective-permute-start(bf16[160,320]{1,0:T(8,128)(2,1)S(1)} %bitcast.818), channel_id=1, source_target_pairs={{0,1},{1,0},{2,3},{3,2},{4,5},{5,4},{6,7},{7,6},{8,9},{9,8},{10,11... | collective-permute-start | bytes 307208 | tf_op jit(solution)/shard_map/ppermute | solution.py:201
  790.6 30.7 %collective-permute-start.74 = (bf16[160,320]{1,0:T(8,128)(2,1)S(1)}, bf16[160,320]{1,0:T(8,128)(2,1)S(1)}, u32[]{:S(2)}, u32[]{:S(2)}) collective-permute-start(bf16[160,320]{1,0:T(8,128)(2,1)S(1)} %bitcast.819), channel_id=1, source_target_pairs={{0,2},{2,0},{1,3},{3,1},{4,6},{6,4},{5,7},{7,5},{8,10},{10,8},{9,1... | collective-permute-start | bytes 307208 | tf_op jit(solution)/shard_map/ppermute | solution.py:201
  791.2 30.1 %collective-permute-start.76 = (bf16[160,320]{1,0:T(8,128)(2,1)}, bf16[160,320]{1,0:T(8,128)(2,1)S(1)}, u32[]{:S(2)}, u32[]{:S(2)}) collective-permute-start(bf16[160,320]{1,0:T(8,128)(2,1)} %collective-permute-done.75), channel_id=1, source_target_pairs={{0,2},{2,0},{1,3},{3,1},{4,6},{6,4},{5,7},{7,5},{8,10},{10,8},{9,1... | collective-permute-start | bytes 307208 | tf_op jit(solution)/shard_map/ppermute | solution.py:201
  821.2 208.4 %reduce-scatter.9.cloned.1.call-start = ((), (), s32[]{:S(2)}) async-start(), calls=%async_computation.11 | async-start | bytes 5529600 | tf_op jit(solution)/shard_map/reduce_scatter | solution.py:770
  857.2 175.2 %reduce-scatter.7.cloned.1.call-start = ((), (), s32[]{:S(2)}) async-start(), calls=%async_computation.10 | async-start | bytes 5529600 | tf_op jit(solution)/shard_map/reduce_scatter | solution.py:770
  886.5 18.1 %collective-permute-start.90 = (bf16[8,320]{1,0:T(8,128)(2,1)S(1)}, bf16[8,320]{1,0:T(8,128)(2,1)S(1)}, u32[]{:S(2)}, u32[]{:S(2)}) collective-permute-start(bf16[8,320]{1,0:T(8,128)(2,1)S(1)} %fusion.190), channel_id=1, source_target_pairs={{0,2},{2,0},{1,3},{3,1},{4,6},{6,4},{5,7},{7,5},{8,10},{10,8},{9,1... | collective-permute-start | bytes 15368 | tf_op jit(solution)/shard_map/ppermute | solution.py:201
  904.6 36.5 %collective-permute-start.91 = (f32[10,320]{1,0:T(8,128)S(1)}, f32[10,320]{1,0:T(8,128)S(1)}, u32[]{:S(2)}, u32[]{:S(2)}) collective-permute-start(f32[10,320]{1,0:T(8,128)S(1)} %pad_maximum_fusion.31), channel_id=1, source_target_pairs={{0,4},{4,0},{1,5},{5,1},{2,6},{6,2},{3,7},{7,3},{8,12},{12,8},{9,1... | collective-permute-start | bytes 38408 | tf_op jit(solution)/shard_map/ppermute | solution.py:201
  947.9 29.8 %collective-permute-start.105 = (bf16[160,2,640]{2,0,1:T(8,128)(2,1)}, bf16[160,2,640]{2,0,1:T(8,128)(2,1)}, u32[]{:S(2)}, u32[]{:S(2)}) collective-permute-start(bf16[160,2,640]{2,0,1:T(8,128)(2,1)} %dynamic-slice_bitcast_fusion.11), channel_id=1, source_target_pairs={{0,4},{4,0},{1,5},{5,1},{2,6},{6,2},{3,7},{7,3},{8,12},{12,8},{9,1... | collective-permute-start | bytes 1228808 | tf_op jit(solution)/shard_map/ppermute | solution.py:201
  (255 other events, 2736.9 us)
Sparse Core Ops, SparseCore 0:
  9.6 90.3 all-gather.6
  102.2 58.5 all-gather.10
  162.4 84.3 all-gather.8
  385.6 35.7 all-gather.14
  428.4 63.3 all-gather.12
  532.7 35.7 reduce-scatter.16
  589.4 60.9 reduce-scatter.14
  774.0 31.5 reduce-scatter.12
  821.3 31.5 reduce-scatter.10
  857.3 78.2 reduce-scatter.8
  941.2 80.0 reduce-scatter.6
